TPU v7x, 32 devices: a whole 2x2x4 slice. The times are simulated.
32 devices in a mesh: resp: 4 (over y, core), ctx: 8 (over z, x).
Axes of the slice: x: 2, y: 2, z: 4, core: 2. Of those that a mesh axis runs over, the one named last changes fastest.
Arguments:
- queries: bfloat16 [8, 2048, 8, 128], P('resp', 'ctx'), may hold values from -170 to 170
- prompt_keys: bfloat16 [128, 128], P('ctx'), may hold values from -6 to 6
- prompt_values: bfloat16 [128, 128], P('ctx'), may hold values from -6 to 6
- resp_keys: bfloat16 [8, 2048, 128], P('resp', 'ctx'), may hold values from -6 to 6
- resp_values: bfloat16 [8, 2048, 128], P('resp', 'ctx'), may hold values from -6 to 6
- upstream: bfloat16 [8, 2048, 8, 128], P('resp', 'ctx'), may hold values from -6 to 6
- behav_logp: float32 [8, 2048], P('resp', 'ctx'), may hold values from -2.5 to -0.1
- cur_logp: float32 [8, 2048], P('resp', 'ctx'), may hold values from -2.5 to -0.1
- advantages: float32 [8], P('resp'), may hold values from -4 to 4
- lengths: int32 [8], P('resp'), may hold values from 128 to 2048, as said below
Outputs:
- grad_queries: bfloat16 [8, 2048, 8, 128], P('resp', 'ctx')
- grad_resp_keys: bfloat16 [8, 2048, 128], P('resp', 'ctx')
- grad_resp_values: bfloat16 [8, 2048, 128], P('resp', 'ctx')
- grad_prompt_keys: float32 [128, 128], P('ctx')
- grad_prompt_values: float32 [128, 128], P('ctx')
Inputs may be any that keep to these rules, and one draw needn't show every extreme that they name: `lengths`: each length is a multiple of 128; in every draw one response has length 2048 and another has length 128.
All inputs are finite; a program needn't handle non-finite values.
Results may differ from a plain program's by a relative error of at most 0.024.
Values may be sent and summed in bfloat16 or wider, within the bound.
No kernel may reach another device: no remote copies, remote signals or barrier semaphores. Data moves between devices by JAX's collectives and lax.ppermute only.
A program may use at most 64 MiB of HBM per device.

v0:
```python
import functools
import math

import jax
import jax.numpy as jnp
from jax import lax
from jax.experimental import pallas as pl
from jax.experimental.pallas import tpu as pltpu
from jax.sharding import PartitionSpec as P

RATIO_CAP = 2.0
MASKED = -1e30
SUB_ROWS = 256
TILE_ROWS = 1024
LARGEST_SCORE = 100.0
UNBOUNDED = 3e38

TOP, TOTAL, DOTTED, GUARD, WEIGHT, LENGTH = range(6)
VMEM_BYTES = 24 * 1024 * 1024
JOIN_VMEM_BYTES = 60 * 1024 * 1024

def dot(a, b):
    return jnp.dot(a, b, preferred_element_type=jnp.float32)


def kinds_of(step, layers):
    if step == 0:
        return ("z",)
    return ("x", "prompt") if step == layers else ("x", "z")


def variants(step, layers, place):
    z, odd = place // 2, place % 2 == 1
    if step == 0:
        return [(None, 0, 1)]
    if step == layers:
        return [(z >= step - 1, 0, 2), (z < step - 1, 1, 2)]
    if step == 1:
        return [
            ((z >= 1) & odd, 0, 2),
            ((z == 0) & odd, 0, 1),
            ((z >= 1) & jnp.logical_not(odd), 1, 2),
        ]
    return [(z >= step, 0, 2), (z == step - 1, 0, 1)]


def attends(step, layers, place):
    if step in (0, layers):
        return place >= 0
    return place >= 1 if step == 1 else place // 2 >= step - 1


def kept_keys(shape, first_row, heads):
    key = lax.broadcasted_iota(jnp.int32, shape, 0)
    row = lax.broadcasted_iota(jnp.int32, shape, 1) + first_row
    return key * heads <= row


def edges_of(counts):
    edges = [0]
    for count in counts:
        edges.append(edges[-1] + count)
    return edges


def largest_norm(rows):
    wide = rows.astype(jnp.float32)
    return jnp.max(jnp.sum(wide * wide, axis=1, keepdims=True))


def filled_tiles(length, tokens, heads, rows):
    per_tile = tile_of(rows) // heads
    left = length - lax.axis_index("ctx") * tokens
    return jnp.clip((left + per_tile - 1) // per_tile, 0, rows // tile_of(rows))


def load_keys(member, pairs, kinds, edges, head_dim, keys, values):
    for part, pair in enumerate(pairs):
        count = edges[part + 1] - edges[part]
        rows = pl.ds(edges[part], count)
        own = pl.ds(0, count)
        if kinds[part] != "prompt":
            own = pl.ds(pl.multiple_of(member * count, count), count)
        keys[rows, :] = pair[own, :head_dim]
        values[rows, :] = pair[own, head_dim:]


def length_of(stat, member):
    return jnp.max(stat[member, LENGTH : LENGTH + 1, 0:128]).astype(jnp.int32)


def spread_weights(ratio, heads):
    tokens = ratio.shape[1]
    shape = (tokens, tokens * heads)
    token = lax.broadcasted_iota(jnp.int32, shape, 0)
    row = lax.broadcasted_iota(jnp.int32, shape, 1)
    first = token * heads
    chosen = jnp.where((row >= first) & (row < first + heads), 1.0, 0.0)
    chosen = chosen.astype(jnp.bfloat16)
    out, rest = None, ratio
    for _ in range(3):
        term = rest.astype(jnp.bfloat16)
        rest = rest - term.astype(jnp.float32)
        few = jnp.broadcast_to(term.astype(jnp.float32), (16, tokens)).astype(jnp.bfloat16)
        part = jnp.dot(few, chosen, preferred_element_type=jnp.float32)[0:1]
        out = part if out is None else out + part
    return out


def key_sum(array):
    count = array.shape[0] // 4
    parts = [
        jnp.sum(array[i * count : (i + 1) * count], axis=0, keepdims=True) for i in range(4)
    ]
    return (parts[0] + parts[1]) + (parts[2] + parts[3])


def prepare_kernel(heads, policy, held_q, held_g, out, q, g, turned_q, turned_g, arrived):
    copies = [
        pltpu.make_async_copy(source, target, arrived.at[i])
        for i, (source, target) in enumerate([(held_q, q), (held_g, g)])
    ]
    for copy in copies:
        copy.start()
    for copy in copies:
        copy.wait()
    members, all_rows, _ = q.shape
    tile = tile_of(all_rows)
    tokens = all_rows // heads
    line = lax.broadcasted_iota(jnp.int32, policy.shape, 0)

    def per_member(member, carry):
        known = jnp.max(jnp.where(line == members + member, policy[...], 0.0))
        out[member, LENGTH : LENGTH + 1, :] = jnp.full((1, all_rows), known)

        def per_tile(index, carry):
            rows = pl.ds(pl.multiple_of(index * tile, tile), tile)
            turned_q[member, :, rows] = q[member, rows, :].T
            turned_g[member, :, rows] = g[member, rows, :].T
            guard = largest_norm(q[member, rows, :])
            out[member, GUARD : GUARD + 1, rows] = jnp.full((1, tile), guard)
            count = tile // heads
            part = pl.ds(pl.multiple_of(index * count, count), count)
            if count == tokens:
                part = pl.ds(0, count)
            chosen = jnp.where(line[:, :count] == member, policy[:, part], 0.0)
            ratio = jnp.sum(chosen, axis=0, keepdims=True)
            out[member, WEIGHT : WEIGHT + 1, rows] = spread_weights(ratio, heads)
            return carry

        filled = filled_tiles(known.astype(jnp.int32), tokens, heads, all_rows)
        lax.fori_loop(0, filled, per_tile, 0)
        return carry

    lax.fori_loop(0, members, per_member, 0)


def forward_kernel(step, layers, heads, head_dim, counts, turned_q, turned_g, earlier, *refs):
    kinds = kinds_of(step, layers)
    parts = len(kinds)
    if step == layers:
        messages, (out, prompt, keys, values) = refs[: 2 * layers], refs[2 * layers :]
        own = messages[0].shape[0] - prompt.shape[0] // (2 * layers)
        each = messages[0].shape[0] - own
        for i, message in enumerate(messages):
            prompt[i * each : (i + 1) * each, :] = message[own:, :]
        pairs = [messages[-1], prompt]
    else:
        pairs, (out, keys, values) = refs[:parts], refs[parts:]
    place = lax.axis_index("ctx")
    members, _, all_rows = turned_q.shape
    tile = tile_of(all_rows)
    tokens = all_rows // heads
    scale = head_dim**-0.5 * math.log2(math.e)
    edges = edges_of(counts)
    attended = attends(step, layers, place)

    def shared(member, low, high, first, start):
        rows = pl.ds(row_start(first, start), SUB_ROWS)
        scores = dot(keys[low:high, :], turned_q[member, :, rows]) * scale
        if step == 0:
            kept = kept_keys(scores.shape, first + start, heads)
            scores = jnp.where(kept, scores, MASKED)
        return rows, scores, dot(values[low:high, :], turned_g[member, :, rows])

    def put(member, first, span, lines):
        rows = pl.ds(first, span)
        for line, pieces in lines.items():
            out[member, line : line + 1, rows] = jnp.concatenate(pieces, 1)

    def bounded(member, low, high, first, span):
        totals, dots = [], []
        for start in range(0, span, SUB_ROWS):
            rows, scores, grad_probs = shared(member, low, high, first, start)
            weight = jnp.exp2(scores)
            total, dotted = key_sum(weight), key_sum(weight * grad_probs)
            if step > 0:
                total = total + earlier[member, TOTAL : TOTAL + 1, rows]
                dotted = dotted + earlier[member, DOTTED : DOTTED + 1, rows]
            totals.append(total)
            dots.append(dotted)
        tops = [jnp.zeros_like(t) for t in totals]
        put(member, first, span, {TOP: tops, TOTAL: totals, DOTTED: dots})

    def general(member, low, high, first, span):
        tops, totals, dots = [], [], []
        for start in range(0, span, SUB_ROWS):
            rows, scores, grad_probs = shared(member, low, high, first, start)
            top = jnp.max(scores, axis=0, keepdims=True)
            if step > 0:
                top = jnp.maximum(top, earlier[member, TOP : TOP + 1, rows])
            weight = jnp.exp2(scores - top)
            total, dotted = key_sum(weight), key_sum(weight * grad_probs)
            if step > 0:
                decay = jnp.exp2(earlier[member, TOP : TOP + 1, rows] - top)
                total = total + decay * earlier[member, TOTAL : TOTAL + 1, rows]
                dotted = dotted + decay * earlier[member, DOTTED : DOTTED + 1, rows]
            tops.append(top)
            totals.append(total)
            dots.append(dotted)
        guards = [jnp.full_like(t, UNBOUNDED) for t in totals]
        put(member, first, span, {TOP: tops, TOTAL: totals, DOTTED: dots, GUARD: guards})

    def per_member(member, carry):
        filled = filled_tiles(length_of(earlier, member), tokens, heads, all_rows)

        @pl.when((filled > 0) & attended)
        def _():
            load_keys(member, pairs, kinds, edges, head_dim, keys, values)
            limit = (LARGEST_SCORE / scale) ** 2 / largest_norm(keys[...])
            guards = earlier[member, GUARD : GUARD + 1, :]
            column = lax.broadcasted_iota(jnp.int32, guards.shape, 1)
            fast = jnp.max(jnp.where(column < filled * tile, guards, 0.0)) <= limit
            for condition, begin, past in variants(step, layers, place):
                low, high = edges[begin], edges[past]
                here = True if condition is None else condition

                @pl.when(fast & here)
                def _():
                    over_tiles(filled, all_rows, functools.partial(bounded, member, low, high))

                @pl.when(jnp.logical_not(fast) & here)
                def _():
                    over_tiles(filled, all_rows, functools.partial(general, member, low, high), 0)

        return carry

    lax.fori_loop(0, members, per_member, 0)


def row_start(first, start):
    if isinstance(first, int):
        return first + start
    return pl.multiple_of(first + start, SUB_ROWS)


def over_tiles(filled, all_rows, body, whole=1):
    tile = tile_of(all_rows)
    tiles = all_rows // tile

    def per_tile(index, carry):
        body(pl.multiple_of(index * tile, tile), tile)
        return carry

    if tiles == 1 or not whole:
        lax.fori_loop(0, filled, per_tile, 0)
        return

    @pl.when(filled == tiles)
    def _():
        body(0, all_rows)

    @pl.when(filled < tiles)
    def _():
        lax.fori_loop(0, filled, per_tile, 0)


def backward_kernel(step, layers, heads, head_dim, counts, *refs):
    q, g, turned_q, turned_g, final = refs[:5]
    refs = refs[5:]
    kinds = kinds_of(step, layers)
    count = len(kinds)
    pairs, refs = refs[:count], refs[count:]
    earlier = None
    if step < layers:
        earlier, refs = refs[0], refs[1:]
    if step == layers - 1:
        stay, leave = refs[:2]
        refs = refs[2:]
    elif step == 1:
        far, refs = refs[0], refs[1:]
    made = 3 if step == layers else count
    grads, query_out, refs = refs[:made], refs[made], refs[made + 1 :]
    keys, values, turned, probs_held, scores_held, sums = refs
    place = lax.axis_index("ctx")
    members, all_rows = q.shape[:2]
    tile = tile_of(all_rows)
    tokens = all_rows // heads
    plain = head_dim**-0.5
    scale = plain * math.log2(math.e)
    edges = edges_of(counts)
    attended = attends(step, layers, place)

    def body(member, low, high, first, span):
        whole = pl.ds(first, span)
        held_rows = slice(0, span)
        total = final[member, TOTAL : TOTAL + 1, whole]
        level = final[member, TOP : TOP + 1, whole] + jnp.log2(total)
        delta = final[member, DOTTED : DOTTED + 1, whole] / total
        token_weight = final[member, WEIGHT : WEIGHT + 1, whole]
        for start in range(0, span, SUB_ROWS):
            rows = pl.ds(row_start(first, start), SUB_ROWS)
            held = slice(start, start + SUB_ROWS)
            scores = dot(keys[low:high, :], turned_q[member, :, rows]) * scale
            scores = scores - level[:, held]
            if step == 0:
                kept = kept_keys(scores.shape, first + start, heads)
                scores = jnp.where(kept, scores, MASKED)
            probs = jnp.exp2(scores) * token_weight[:, held]
            grad_probs = dot(values[low:high, :], turned_g[member, :, rows])
            grad_scores = probs * (grad_probs - delta[:, held])
            probs_held[low:high, held] = probs.astype(jnp.bfloat16)
            scores_held[low:high, held] = grad_scores.astype(jnp.bfloat16)
        sums[low:high, head_dim:] += dot(probs_held[low:high, held_rows], g[member, whole, :])
        sums[low:high, :head_dim] += dot(scores_held[low:high, held_rows], q[member, whole, :])
        moved = dot(turned[:, low:high], scores_held[low:high, held_rows])
        if earlier is not None:
            moved = moved + earlier[member, :, whole]
        if step == 0:
            query_out[member, whole, :] = (moved * plain).T.astype(jnp.bfloat16)
        else:
            query_out[member, :, whole] = moved

    def per_member(member, carry):
        filled = filled_tiles(length_of(final, member), tokens, heads, all_rows)
        filled = jnp.where(attended, filled, 0)
        for part in range(count):
            rows = pl.ds(edges[part], edges[part + 1] - edges[part])

            @pl.when((member == 0) | (kinds[part] != "prompt"))
            def _():
                sums[rows, :] = jnp.zeros_like(sums[rows, :])

        @pl.when(filled > 0)
        def _():
            load_keys(member, pairs, kinds, edges, head_dim, keys, values)
            turned[...] = keys[...].T

            for condition, begin, past in variants(step, layers, place):
                low, high = edges[begin], edges[past]

                @pl.when(True if condition is None else condition)
                def _():
                    over_tiles(filled, all_rows, functools.partial(body, member, low, high), 0)

        if step == 0 or earlier is None:

            def clear(index, carry):
                rows = pl.ds(pl.multiple_of(index * tile, tile), tile)
                if step == 0:
                    query_out[member, rows, :] = jnp.zeros((tile, head_dim), jnp.bfloat16)
                else:
                    query_out[member, :, rows] = jnp.zeros((head_dim, tile), jnp.float32)
                return carry

            lax.fori_loop(filled, all_rows // tile, clear, 0)
        for part in range(count):
            if kinds[part] == "prompt":
                continue
            rows = pl.ds(edges[part], counts[part])
            own = pl.ds(pl.multiple_of(member * counts[part], counts[part]), counts[part])
            key_part, value_part = sums[rows, :head_dim] * plain, sums[rows, head_dim:]
            if step == 1 and part == 0:
                key_part = key_part + far[own, :head_dim].astype(jnp.float32)
                value_part = value_part + far[own, head_dim:].astype(jnp.float32)
            grads[part][own, :head_dim] = key_part.astype(jnp.bfloat16)
            grads[part][own, head_dim:] = value_part.astype(jnp.bfloat16)
        return carry

    lax.fori_loop(0, members, per_member, 0)
    tail = members * tokens
    if step == layers:
        far, stay, leave = grads
        middle = edges[1] + stay.shape[0]
        last = middle + leave.shape[0]
        for target, begin, rows in (
            (stay, 0, slice(edges[1], middle)),
            (leave, 0, slice(middle, last)),
            (far, tail, slice(last, edges[2])),
        ):
            end = target.shape[0]
            target[begin:end, :head_dim] = (sums[rows, :head_dim] * plain).astype(target.dtype)
            target[begin:end, head_dim:] = sums[rows, head_dim:].astype(target.dtype)
    elif step == layers - 1:
        grads[0][tail:, :] = leave[...]
        grads[1][tail:, :] = stay[leave.shape[0] :, :].astype(jnp.bfloat16)
    elif step == 1:
        grads[0][tail:, :] = far[tail:, :]


def combine_kernel(step, layers, each, own, side, above, kept, *refs):
    def wide(ref, rows):
        return ref[rows, :].astype(jnp.float32)

    count = own.shape[0]
    rows = slice(0, count)
    mine = slice(step * each, (step + 1) * each)
    prompt = kept[mine, :] + wide(above, slice(count, None))
    if step == layers - 2:
        prompt = prompt + wide(side, slice(count + mine.start, count + mine.stop))
    total = wide(own, rows) + wide(side, rows) + wide(above, rows)
    if step > 0:
        out = refs[0]
        out[rows, :] = total.astype(jnp.bfloat16)
        out[count:, :] = prompt.astype(jnp.bfloat16)
        if step == layers - 2:
            refs[1][...] = kept[: step * each, :] + wide(side, slice(count, count + step * each))
    else:
        key_out, value_out, prompt_out = refs
        total = total.astype(jnp.bfloat16)
        head_dim = key_out.shape[1]
        key_out[...] = total[:, :head_dim]
        value_out[...] = total[:, head_dim:]
        prompt_out[...] = prompt + wide(side, slice(count, None))


def tile_of(rows):
    return min(TILE_ROWS, rows)


WHOLE = pl.BlockSpec(memory_space=pltpu.VMEM)
PARAMS = pltpu.CompilerParams(vmem_limit_bytes=VMEM_BYTES)
LITTLE = pl.CostEstimate(flops=1000, bytes_accessed=1000, transcendentals=0)


OUTSIDE = pl.BlockSpec(memory_space=pltpu.HBM)


def prepare(heads, policy, q, g):
    members, rows, head_dim = q.shape
    turned = jax.ShapeDtypeStruct((members, head_dim, rows), q.dtype)
    return pl.pallas_call(
        functools.partial(prepare_kernel, heads),
        in_specs=[WHOLE] + [OUTSIDE] * 2,
        out_specs=[WHOLE] * 5,
        out_shape=[jax.ShapeDtypeStruct((members, 8, rows), jnp.float32)]
        + [jax.ShapeDtypeStruct(q.shape, q.dtype)] * 2
        + [turned] * 2,
        scratch_shapes=[pltpu.SemaphoreType.DMA((2,))],
        compiler_params=PARAMS,
        cost_estimate=LITTLE,
        name="prepare_rows",
    )(policy, q, g)


def forward_step(step, layers, heads, tokens, turned, earlier, messages):
    members, head_dim, rows = turned[0].shape
    each = messages[0].shape[0] - members * tokens
    counts = [tokens] * len(kinds_of(step, layers))
    out_shape = [jax.ShapeDtypeStruct((members, 8, rows), jnp.float32)]
    if step == layers:
        counts[1] = 2 * layers * each
        out_shape.append(jax.ShapeDtypeStruct((counts[1], 2 * head_dim), jnp.bfloat16))
    return pl.pallas_call(
        functools.partial(forward_kernel, step, layers, heads, head_dim, counts),
        in_specs=[WHOLE] * (3 + len(messages)),
        out_specs=[WHOLE] * len(out_shape),
        out_shape=out_shape,
        scratch_shapes=[pltpu.VMEM((sum(counts), head_dim), jnp.bfloat16)] * 2,
        compiler_params=PARAMS,
        cost_estimate=LITTLE,
        input_output_aliases={2: 0},
        name=f"attend_step{step}",
    )(*turned, earlier, *messages)


def backward_step(
    step, layers, heads, tokens, each, held_rows, final, messages, earlier, prompt_terms
):
    q = held_rows[0]
    members, rows, head_dim = q.shape
    counts = [tokens] * len(kinds_of(step, layers))

    def block(more, dtype=jnp.bfloat16, base=members * tokens):
        return jax.ShapeDtypeStruct((base + more, 2 * head_dim), dtype)

    if step == layers:
        counts[1] = 2 * layers * each
        grad_shapes = [
            block(each),
            block(layers * each, jnp.float32, 0),
            block((layers - 1) * each, jnp.bfloat16, 0),
        ]
    elif step == layers - 1:
        grad_shapes = [block((layers - 1) * each), block(each)]
    elif step == 1:
        grad_shapes = [block(each), block(0)]
    else:
        grad_shapes = [block(0)] * len(counts)
    columns = sum(counts)
    if step == 0:
        query_shape = jax.ShapeDtypeStruct(q.shape, jnp.bfloat16)
    else:
        query_shape = jax.ShapeDtypeStruct((members, head_dim, rows), jnp.float32)
    extra = [] if earlier is None else [earlier]
    aliases = {5 + len(messages): len(grad_shapes)} if extra and step > 0 else {}
    extra += prompt_terms
    outs = pl.pallas_call(
        functools.partial(backward_kernel, step, layers, heads, head_dim, counts),
        in_specs=[WHOLE] * (5 + len(messages) + len(extra)),
        out_specs=[WHOLE] * (len(grad_shapes) + 1),
        out_shape=grad_shapes + [query_shape],
        scratch_shapes=[pltpu.VMEM((columns, head_dim), jnp.bfloat16)] * 2
        + [pltpu.VMEM((head_dim, columns), jnp.bfloat16)]
        + [pltpu.VMEM((columns, tile_of(rows)), jnp.bfloat16)] * 2
        + [pltpu.VMEM((columns, 2 * head_dim), jnp.float32)],
        compiler_params=PARAMS,
        cost_estimate=LITTLE,
        input_output_aliases=aliases,
        name=f"attend_grad_step{step}",
    )(*held_rows, final, *messages, *extra)
    return outs[:-1], outs[-1]


def combine(step, layers, each, *terms):
    count, width = terms[0].shape
    if step > 0:
        shapes = [jax.ShapeDtypeStruct((count + each, width), jnp.bfloat16)]
        if step == layers - 2:
            shapes.append(jax.ShapeDtypeStruct((step * each, width), jnp.float32))
    else:
        shapes = [jax.ShapeDtypeStruct((count, width // 2), jnp.bfloat16)] * 2
        shapes.append(jax.ShapeDtypeStruct((each, width), jnp.float32))
    return pl.pallas_call(
        functools.partial(combine_kernel, step, layers, each),
        in_specs=[WHOLE] * len(terms),
        out_specs=[WHOLE] * len(shapes),
        out_shape=shapes,
        compiler_params=PARAMS,
        name=f"add_terms{step}",
    )(*terms)


def join_kernel(
    keys, values, prompt_keys, prompt_values, behaved, current, advantages, lengths, *refs
):
    out, policy, held_behaved, held_current, held_advantages, held_lengths, arrived = refs
    rows, head_dim = keys.shape
    members, tokens = behaved.shape

    def part(first, count, column):
        return out.at[pl.ds(first, count), pl.ds(column, head_dim)]

    each = prompt_keys.shape[0]
    targets = [
        (keys, part(0, rows, 0)),
        (values, part(0, rows, head_dim)),
        (prompt_keys, part(rows, each, 0)),
        (prompt_values, part(rows, each, head_dim)),
        (behaved, held_behaved),
        (current, held_current),
        (advantages, held_advantages),
        (lengths, held_lengths),
    ]
    copies = [
        pltpu.make_async_copy(source, target, arrived.at[i])
        for i, (source, target) in enumerate(targets)
    ]
    for copy in copies:
        copy.start()
    for copy in copies:
        copy.wait()
    full_len = tokens * lax.axis_size("ctx")
    position = lax.axis_index("ctx") * tokens + lax.broadcasted_iota(jnp.int32, (1, tokens), 1)
    ratio = jnp.minimum(jnp.exp(held_current[...] - held_behaved[...]), RATIO_CAP)
    for member in range(members):
        length = held_lengths[member]
        spread = full_len / jnp.full((1, 1), length).astype(jnp.float32)
        valid = jnp.where(position < length, ratio[member : member + 1], 0.0)
        policy[member : member + 1, :] = -held_advantages[member] * valid * spread
        wide = jnp.full((1, tokens), length).astype(jnp.float32)
        policy[members + member : members + member + 1, :] = wide


def join(keys, values, prompt_keys, prompt_values, behaved, current, advantages, lengths):
    rows = keys.shape[0] + prompt_keys.shape[0]
    members, tokens = behaved.shape
    return pl.pallas_call(
        join_kernel,
        out_shape=[
            jax.ShapeDtypeStruct((rows, 2 * keys.shape[1]), keys.dtype),
            jax.ShapeDtypeStruct((2 * members, tokens), jnp.float32),
        ],
        in_specs=[OUTSIDE] * 8,
        out_specs=[WHOLE] * 2,
        scratch_shapes=[
            pltpu.VMEM((members, tokens), jnp.float32),
            pltpu.VMEM((members, tokens), jnp.float32),
            pltpu.SMEM((members,), jnp.float32),
            pltpu.SMEM((members,), jnp.int32),
            pltpu.SemaphoreType.DMA((8,)),
        ],
        compiler_params=pltpu.CompilerParams(vmem_limit_bytes=JOIN_VMEM_BYTES),
        cost_estimate=LITTLE,
        name="join_pairs",
    )(keys, values, prompt_keys, prompt_values, behaved, current, advantages, lengths)


def per_device(
    queries,
    prompt_keys,
    prompt_values,
    resp_keys,
    resp_values,
    upstream,
    behav_logp,
    cur_logp,
    advantages,
    lengths,
):
    members, tokens, heads, head_dim = queries.shape
    ctx_size, resp_size = lax.axis_size("ctx"), lax.axis_size("resp")
    layers = ctx_size // 2
    each = prompt_keys.shape[0]
    rows = tokens * heads

    def hop(array, layers_up):
        pairs = [(c, (c + 2 * layers_up) % ctx_size) for c in range(ctx_size)]
        return lax.ppermute(array, "ctx", pairs)

    def cross(array):
        return lax.ppermute(array, "ctx", [(c, c ^ 1) for c in range(ctx_size)])

    own, policy = join(
        resp_keys.reshape(members * tokens, head_dim),
        resp_values.reshape(members * tokens, head_dim),
        prompt_keys,
        prompt_values,
        behav_logp,
        cur_logp,
        advantages,
        lengths,
    )
    z, x = [own, hop(own, 1)], [None, cross(own)]
    stat, *held_rows = prepare(
        heads,
        policy,
        queries.reshape(members, rows, head_dim),
        upstream.reshape(members, rows, head_dim),
    )

    def forward(step, stat, messages):
        return forward_step(step, layers, heads, tokens, held_rows[2:], stat, messages)

    for step in range(1, layers):
        z[step], stat = lax.optimization_barrier((z[step], stat))
        if step + 1 < layers:
            z.append(hop(z[step], 1))
            x.append(cross(z[step]))
        else:
            x.append(hop(x[1], layers - 1))
        if step == 1:
            (stat,) = forward(0, stat, z[:1])
        (stat,) = forward(step, stat, [x[step], z[step]])
    stat, prompt = forward(layers, stat, z + x[1:])
    final = stat
    moved = side = above = far = message = kept = None
    terms = []
    for step in range(layers, -1, -1):
        if message is not None:
            final, message = lax.optimization_barrier((final, message))
            above = hop(message, -1)
        if step == layers:
            messages = [x[step], prompt]
        else:
            messages = [z[0]] if step == 0 else [x[step], z[step]]
        grads, moved = backward_step(
            step, layers, heads, tokens, each, held_rows, final, messages, moved, terms
        )
        terms = [far] if step == 2 else []
        if step == layers:
            far, terms = hop(grads[0], 1 - layers), list(grads[1:])
            kept = grads[1]
        elif step == layers - 1:
            message = grads[1]
        elif step > 0:
            message, *more = combine(step, layers, each, grads[-1], side, above, kept)
            kept = more[0] if more else kept
        if 0 < step < layers:
            side = cross(grads[0])
    key_grads, value_grads, share = combine(0, layers, each, grads[-1], side, above, kept)
    stride = 1
    while stride < resp_size:
        pairs = [(c, c ^ stride) for c in range(resp_size)]
        share = share + lax.ppermute(share, "resp", pairs)
        stride *= 2
    return (
        moved.reshape(queries.shape),
        key_grads.reshape(resp_keys.shape),
        value_grads.reshape(resp_values.shape),
        share[:, :head_dim],
        share[:, head_dim:],
    )


def solution(mesh):
    placed = (
        P("resp", "ctx", None, None),
        P("ctx", None),
        P("ctx", None),
        P("resp", "ctx", None),
        P("resp", "ctx", None),
        P("resp", "ctx", None, None),
        P("resp", "ctx"),
        P("resp", "ctx"),
        P("resp"),
        P("resp"),
    )
    return jax.shard_map(
        per_device,
        mesh=mesh,
        in_specs=placed,
        out_specs=(
            P("resp", "ctx", None, None),
            P("resp", "ctx", None),
            P("resp", "ctx", None),
            P("ctx", None),
            P("ctx", None),
        ),
        check_vma=False,
    )
```

profile of v0, /device:TPU:0, one launch (start us, length us, event | category | flops | bytes accessed | tf_op | source)
XLA Modules:
  0.0 78.8 jit_solution(16925235848562918372)
XLA Ops:
  0.6 1.8 %join_pairs.1 = (bf16[528,256]{1,0:T(8,128)(2,1)}, f32[4,256]{1,0:T(4,128)}) custom-call(bf16[512,128]{1,0:T(8,128)(2,1)} %bitcast.9, bf16[512,128]{1,0:T(8,128)(2,1)} %bitcast.10, bf16[16,128]{1,0:T(8,128)(2,1)} %prompt_keys.1, bf16[16,128]{1,0:T(8,128)(2,1)} %prompt_values.1, f32[2,256]{1,0:T(2,128)} %behaved.1, f32[2,256]{1,0:T(2,128)} %current.1, ...), custom_call_target="tpu_custom_call" | custom-call | flops 1000 | bytes 1000 | tf_op jit(solution)/shard_map/join_pairs/pallas_call | solution.py:588
  2.4 0.0 copy-start
  2.4 3.1 %collective-permute-start = (bf16[528,256]{1,0:T(8,128)(2,1)}, bf16[528,256]{1,0:T(8,128)(2,1)S(1)}, u32[]{:S(2)}, u32[]{:S(2)}) collective-permute-start(bf16[528,256]{1,0:T(8,128)(2,1)} %get-tuple-element.51.refs_0_.refs_5_), channel_id=1, source_target_pairs={{0,2},{1,3},{2,4},{3,5},{4,6},{5,7},{6,0},{7,1},{8,10},{9,11},{10,... | collective-permute-start | bytes 811016 | tf_op jit(solution)/shard_map/ppermute | solution.py:629
  5.5 1.5 %collective-permute-start.2 = (bf16[528,256]{1,0:T(8,128)(2,1)}, bf16[528,256]{1,0:T(8,128)(2,1)S(1)}, u32[]{:S(2)}, u32[]{:S(2)}) collective-permute-start(bf16[528,256]{1,0:T(8,128)(2,1)} %get-tuple-element.51.refs_0_.refs_5_), channel_id=1, source_target_pairs={{0,1},{1,0},{2,3},{3,2},{4,5},{5,4},{6,7},{7,6},{8,9},{9,8},{10,11... | collective-permute-start | bytes 811016 | tf_op jit(solution)/shard_map/ppermute | solution.py:632
  7.0 1.2 %copy-done.1 = bf16[2,256,8,128]{3,2,1,0:T(8,128)(2,1)S(1)} copy-done((bf16[2,256,8,128]{3,2,1,0:T(8,128)(2,1)S(1)}, bf16[2,256,8,128]{3,2,1,0:T(8,128)(2,1)}, u32[]{:S(2)}) %copy-start.1) | copy-done | bytes 1048600
  8.2 1.2 %copy-done.2 = bf16[2,256,8,128]{3,2,1,0:T(8,128)(2,1)S(1)} copy-done((bf16[2,256,8,128]{3,2,1,0:T(8,128)(2,1)S(1)}, bf16[2,256,8,128]{3,2,1,0:T(8,128)(2,1)}, u32[]{:S(2)}) %copy-start.2) | copy-done | bytes 1048600
  9.4 0.7 copy-done.3
  10.1 2.2 %prepare_rows.1 = (f32[2,8,2048]{2,1,0:T(8,128)S(1)}, bf16[2,2048,128]{2,1,0:T(8,128)(2,1)S(1)}, bf16[2,2048,128]{2,1,0:T(8,128)(2,1)S(1)}, bf16[2,128,2048]{2,1,0:T(8,128)(2,1)S(1)}, bf16[2,128,2048]{2,1,0:T(8,128)(2,1)S(1)}) custom-call(f32[4,256]{1,0:T(4,128)S(1)} %copy-done.3, bf16[2,2048,128]{2,1,0:T(8,128)(2,1)S(1)} %bitcast.7, ...), custom_call_target="tpu_custom_call" | custom-call | flops 1000 | bytes 1000 | tf_op jit(solution)/shard_map/prepare_rows/pallas_call | solution.py:442
  12.4 1.9 %collective-permute-done.refs_1_.refs_6_ = bf16[528,256]{1,0:T(8,128)(2,1)S(1)} collective-permute-done((bf16[528,256]{1,0:T(8,128)(2,1)}, bf16[528,256]{1,0:T(8,128)(2,1)S(1)}, u32[]{:S(2)}, u32[]{:S(2)}) %collective-permute-start) | collective-permute-done | bytes 270368 | tf_op jit(solution)/shard_map/ppermute | solution.py:629
  14.2 0.0 collective-permute-start.1
  14.2 1.5 %collective-permute-start.4 = (bf16[528,256]{1,0:T(8,128)(2,1)S(1)}, bf16[528,256]{1,0:T(8,128)(2,1)S(1)}, u32[]{:S(2)}, u32[]{:S(2)}) collective-permute-start(bf16[528,256]{1,0:T(8,128)(2,1)S(1)} %collective-permute-done.refs_1_.refs_6_), channel_id=1, source_target_pairs={{0,1},{1,0},{2,3},{3,2},{4,5},{5,4},{6,7},{7,6},{8,9},{9,8},{10,11... | collective-permute-start | bytes 811016 | tf_op jit(solution)/shard_map/ppermute | solution.py:632
  15.7 3.1 %attend_step0.1.earlier = f32[2,8,2048]{2,1,0:T(8,128)S(1)} custom-call(bf16[2,128,2048]{2,1,0:T(8,128)(2,1)S(1)} %get-tuple-element.49.turned_q.refs_2_, bf16[2,128,2048]{2,1,0:T(8,128)(2,1)S(1)} %get-tuple-element.50.turned_g.refs_3_, f32[2,8,2048]{2,1,0:T(8,128)S(1)} %get-tuple-element.54.earlier, ...), custom_call_target="tpu_custom_call", output_to_operand_aliasing={{}: (2, {})} | custom-call | flops 1000 | bytes 1000 | tf_op jit(solution)/shard_map/attend_step0/pallas_call | solution.py:464
  18.8 0.0 collective-permute-done.2.refs_0_.refs_4_.refs_5_
  18.8 0.3 attend_step1.1.earlier
  19.1 4.6 %collective-permute-done.1.refs_1_.refs_2_.refs_6_ = bf16[528,256]{1,0:T(8,128)(2,1)S(1)} collective-permute-done((bf16[528,256]{1,0:T(8,128)(2,1)S(1)}, bf16[528,256]{1,0:T(8,128)(2,1)S(1)}, u32[]{:S(2)}, u32[]{:S(2)}) %collective-permute-start.1) | collective-permute-done | bytes 270368 | tf_op jit(solution)/shard_map/ppermute | solution.py:629
  23.7 0.0 collective-permute-start.3
  23.7 2.1 %collective-permute-start.5 = (bf16[528,256]{1,0:T(8,128)(2,1)S(1)}, bf16[528,256]{1,0:T(8,128)(2,1)S(1)}, u32[]{:S(2)}, u32[]{:S(2)}) collective-permute-start(bf16[528,256]{1,0:T(8,128)(2,1)S(1)} %collective-permute-done.1.refs_1_.refs_2_.refs_6_), channel_id=1, source_target_pairs={{0,1},{1,0},{2,3},{3,2},{4,5},{5,4},{6,7},{7,6},{8,9},{9,8},{10,11... | collective-permute-start | bytes 811016 | tf_op jit(solution)/shard_map/ppermute | solution.py:632
  25.8 3.0 %collective-permute-start.6 = (bf16[528,256]{1,0:T(8,128)(2,1)S(1)}, bf16[528,256]{1,0:T(8,128)(2,1)S(1)}, u32[]{:S(2)}, u32[]{:S(2)}) collective-permute-start(bf16[528,256]{1,0:T(8,128)(2,1)S(1)} %collective-permute-done.2.refs_0_.refs_4_.refs_5_), channel_id=1, source_target_pairs={{0,6},{1,7},{2,0},{3,1},{4,2},{5,3},{6,4},{7,5},{8,14},{9,15},{10,... | collective-permute-start | bytes 811016 | tf_op jit(solution)/shard_map/ppermute | solution.py:629
  28.8 0.0 collective-permute-done.4.refs_0_.refs_5_
  28.8 0.3 attend_step2.1.earlier
  29.1 5.8 %collective-permute-done.3.refs_1_.refs_3_.refs_6_ = bf16[528,256]{1,0:T(8,128)(2,1)S(1)} collective-permute-done((bf16[528,256]{1,0:T(8,128)(2,1)S(1)}, bf16[528,256]{1,0:T(8,128)(2,1)S(1)}, u32[]{:S(2)}, u32[]{:S(2)}) %collective-permute-start.3) | collective-permute-done | bytes 270368 | tf_op jit(solution)/shard_map/ppermute | solution.py:629
  34.9 0.0 collective-permute-done.5.refs_0_.refs_6_.refs_5_
  34.9 0.3 attend_step3.1.earlier
  35.2 1.8 %collective-permute-done.6.refs_7_.refs_5_ = bf16[528,256]{1,0:T(8,128)(2,1)S(1)} collective-permute-done((bf16[528,256]{1,0:T(8,128)(2,1)S(1)}, bf16[528,256]{1,0:T(8,128)(2,1)S(1)}, u32[]{:S(2)}, u32[]{:S(2)}) %collective-permute-start.6) | collective-permute-done | bytes 270368 | tf_op jit(solution)/shard_map/ppermute | solution.py:629
  37.0 2.3 %attend_step4.1 = (f32[2,8,2048]{2,1,0:T(8,128)S(1)}, bf16[128,256]{1,0:T(8,128)(2,1)S(1)}) custom-call(bf16[2,128,2048]{2,1,0:T(8,128)(2,1)S(1)} %get-tuple-element.49.turned_q.refs_2_, bf16[2,128,2048]{2,1,0:T(8,128)(2,1)S(1)} %get-tuple-element.50.turned_g.refs_3_, f32[2,8,2048]{2,1,0:T(8,128)S(1)} %attend_step3.1.earlier, ...), custom_call_target="tpu_custom_call", output_to_operand_aliasing={{0}: (2, {})} | custom-call | flops 1000 | bytes 1000 | tf_op jit(solution)/shard_map/attend_step4/pallas_call | solution.py:464
  39.3 2.8 %attend_grad_step4.1 = (bf16[528,256]{1,0:T(8,128)(2,1)S(1)}, f32[64,256]{1,0:T(8,128)S(1)}, bf16[48,256]{1,0:T(8,128)(2,1)S(1)}, f32[2,128,2048]{2,1,0:T(8,128)S(1)}) custom-call(bf16[2,2048,128]{2,1,0:T(8,128)(2,1)S(1)} %get-tuple-element.47.refs_0_, bf16[2,2048,128]{2,1,0:T(8,128)(2,1)S(1)} %get-tuple-element.48.refs_1_, ...), custom_call_target="tpu_custom_call" | custom-call | flops 1000 | bytes 1000 | tf_op jit(solution)/shard_map/attend_grad_step4/pallas_call | solution.py:508
  42.1 0.4 attend_grad_step3.1
  42.5 1.1 %collective-permute-start.7 = (bf16[560,256]{1,0:T(8,128)(2,1)S(1)}, bf16[560,256]{1,0:T(8,128)(2,1)S(1)}, u32[]{:S(2)}, u32[]{:S(2)}) collective-permute-start(bf16[560,256]{1,0:T(8,128)(2,1)S(1)} %get-tuple-element.68), channel_id=1, source_target_pairs={{0,1},{1,0},{2,3},{3,2},{4,5},{5,4},{6,7},{7,6},{8,9},{9,8},{10,11... | collective-permute-start | bytes 860168 | tf_op jit(solution)/shard_map/ppermute | solution.py:632
  43.5 0.0 collective-permute-start.8
  43.5 2.0 %collective-permute-start.9 = (bf16[528,256]{1,0:T(8,128)(2,1)S(1)}, bf16[528,256]{1,0:T(8,128)(2,1)S(1)}, u32[]{:S(2)}, u32[]{:S(2)}) collective-permute-start(bf16[528,256]{1,0:T(8,128)(2,1)S(1)} %get-tuple-element.73), channel_id=1, source_target_pairs={{0,2},{1,3},{2,4},{3,5},{4,6},{5,7},{6,0},{7,1},{8,10},{9,11},{10,... | collective-permute-start | bytes 811016 | tf_op jit(solution)/shard_map/ppermute | solution.py:629
  45.6 0.3 attend_grad_step2.1
  45.9 5.9 %collective-permute-done.8.above = bf16[528,256]{1,0:T(8,128)(2,1)S(1)} collective-permute-done((bf16[528,256]{1,0:T(8,128)(2,1)S(1)}, bf16[528,256]{1,0:T(8,128)(2,1)S(1)}, u32[]{:S(2)}, u32[]{:S(2)}) %collective-permute-start.8) | collective-permute-done | bytes 270368 | tf_op jit(solution)/shard_map/ppermute | solution.py:629
  51.8 0.1 add_terms2.1
  51.9 2.6 %collective-permute-start.11 = (bf16[528,256]{1,0:T(8,128)(2,1)S(1)}, bf16[528,256]{1,0:T(8,128)(2,1)S(1)}, u32[]{:S(2)}, u32[]{:S(2)}) collective-permute-start(bf16[528,256]{1,0:T(8,128)(2,1)S(1)} %get-tuple-element.76), channel_id=1, source_target_pairs={{0,6},{1,7},{2,0},{3,1},{4,2},{5,3},{6,4},{7,5},{8,14},{9,15},{10,... | collective-permute-start | bytes 811016 | tf_op jit(solution)/shard_map/ppermute | solution.py:629
  54.5 1.7 %collective-permute-start.10 = (bf16[512,256]{1,0:T(8,128)(2,1)S(1)}, bf16[512,256]{1,0:T(8,128)(2,1)S(1)}, u32[]{:S(2)}, u32[]{:S(2)}) collective-permute-start(bf16[512,256]{1,0:T(8,128)(2,1)S(1)} %get-tuple-element.75), channel_id=1, source_target_pairs={{0,1},{1,0},{2,3},{3,2},{4,5},{5,4},{6,7},{7,6},{8,9},{9,8},{10,11... | collective-permute-start | bytes 786440 | tf_op jit(solution)/shard_map/ppermute | solution.py:632
  56.2 1.7 %collective-permute-done.9.refs_8_ = bf16[528,256]{1,0:T(8,128)(2,1)S(1)} collective-permute-done((bf16[528,256]{1,0:T(8,128)(2,1)S(1)}, bf16[528,256]{1,0:T(8,128)(2,1)S(1)}, u32[]{:S(2)}, u32[]{:S(2)}) %collective-permute-start.9) | collective-permute-done | bytes 270368 | tf_op jit(solution)/shard_map/ppermute | solution.py:629
  57.9 0.4 attend_grad_step1.1
  58.3 5.1 %collective-permute-start.12 = (bf16[528,256]{1,0:T(8,128)(2,1)S(1)}, bf16[528,256]{1,0:T(8,128)(2,1)S(1)}, u32[]{:S(2)}, u32[]{:S(2)}) collective-permute-start(bf16[528,256]{1,0:T(8,128)(2,1)S(1)} %get-tuple-element.82), channel_id=1, source_target_pairs={{0,1},{1,0},{2,3},{3,2},{4,5},{5,4},{6,7},{7,6},{8,9},{9,8},{10,11... | collective-permute-start | bytes 811016 | tf_op jit(solution)/shard_map/ppermute | solution.py:632
  63.3 0.1 add_terms1.1
  63.4 0.5 collective-permute-start.13
  63.9 5.0 %attend_grad_step0.1 = (bf16[512,256]{1,0:T(8,128)(2,1)S(1)}, bf16[2,2048,128]{2,1,0:T(8,128)(2,1)}) custom-call(bf16[2,2048,128]{2,1,0:T(8,128)(2,1)S(1)} %get-tuple-element.47.refs_0_, bf16[2,2048,128]{2,1,0:T(8,128)(2,1)S(1)} %get-tuple-element.48.refs_1_, bf16[2,128,2048]{2,1,0:T(8,128)(2,1)S(1)} %get-tuple-element.49.turned_q.refs_2_, ...), custom_call_target="tpu_custom_call" | custom-call | flops 1000 | bytes 1000 | tf_op jit(solution)/shard_map/attend_grad_step0/pallas_call | solution.py:508
  68.9 1.0 %collective-permute-done.13.above = bf16[528,256]{1,0:T(8,128)(2,1)S(1)} collective-permute-done((bf16[528,256]{1,0:T(8,128)(2,1)S(1)}, bf16[528,256]{1,0:T(8,128)(2,1)S(1)}, u32[]{:S(2)}, u32[]{:S(2)}) %collective-permute-start.13) | collective-permute-done | bytes 270368 | tf_op jit(solution)/shard_map/ppermute | solution.py:629
  69.9 0.8 add_terms0.1
  70.7 0.0 collective-permute-start.14
  70.7 1.2 %collective-permute-done.14 = f32[16,256]{1,0:T(8,128)S(1)} collective-permute-done((f32[16,256]{1,0:T(8,128)S(1)}, f32[16,256]{1,0:T(8,128)S(1)}, u32[]{:S(2)}, u32[]{:S(2)}) %collective-permute-start.14) | collective-permute-done | bytes 16416 | tf_op jit(solution)/shard_map/ppermute | solution.py:695
  71.9 4.6 %collective-permute-start.15 = (f32[16,256]{1,0:T(8,128)S(1)}, f32[16,256]{1,0:T(8,128)S(1)}, u32[]{:S(2)}, u32[]{:S(2)}) collective-permute-start(f32[16,256]{1,0:T(8,128)S(1)} %add.6), channel_id=1, source_target_pairs={{0,16},{8,24},{16,0},{24,8},{1,17},{9,25},{17,1},{25,9},{2,18},{10... | collective-permute-start | bytes 49160 | tf_op jit(solution)/shard_map/ppermute | solution.py:695
  76.5 1.7 %collective-permute-done.15 = f32[16,256]{1,0:T(8,128)S(1)} collective-permute-done((f32[16,256]{1,0:T(8,128)S(1)}, f32[16,256]{1,0:T(8,128)S(1)}, u32[]{:S(2)}, u32[]{:S(2)}) %collective-permute-start.15) | collective-permute-done | bytes 16416 | tf_op jit(solution)/shard_map/ppermute | solution.py:695
  78.2 0.6 fusion
  (10 shorter events, 0.0 us)
Async XLA Ops:
  2.4 13.3 %copy-start = (bf16[528,256]{1,0:T(8,128)(2,1)S(1)}, bf16[528,256]{1,0:T(8,128)(2,1)}, u32[]{:S(2)}) copy-start(bf16[528,256]{1,0:T(8,128)(2,1)} %get-tuple-element.51.refs_0_.refs_5_) | copy-start | bytes 811012
  2.4 11.8 %collective-permute-start = (bf16[528,256]{1,0:T(8,128)(2,1)}, bf16[528,256]{1,0:T(8,128)(2,1)S(1)}, u32[]{:S(2)}, u32[]{:S(2)}) collective-permute-start(bf16[528,256]{1,0:T(8,128)(2,1)} %get-tuple-element.51.refs_0_.refs_5_), channel_id=1, source_target_pairs={{0,2},{1,3},{2,4},{3,5},{4,6},{5,7},{6,0},{7,1},{8,10},{9,11},{10,... | collective-permute-start | bytes 811016 | tf_op jit(solution)/shard_map/ppermute | solution.py:629
  5.5 13.3 %collective-permute-start.2 = (bf16[528,256]{1,0:T(8,128)(2,1)}, bf16[528,256]{1,0:T(8,128)(2,1)S(1)}, u32[]{:S(2)}, u32[]{:S(2)}) collective-permute-start(bf16[528,256]{1,0:T(8,128)(2,1)} %get-tuple-element.51.refs_0_.refs_5_), channel_id=1, source_target_pairs={{0,1},{1,0},{2,3},{3,2},{4,5},{5,4},{6,7},{7,6},{8,9},{9,8},{10,11... | collective-permute-start | bytes 811016 | tf_op jit(solution)/shard_map/ppermute | solution.py:632
  7.0 1.2 %copy-start.1 = (bf16[2,256,8,128]{3,2,1,0:T(8,128)(2,1)S(1)}, bf16[2,256,8,128]{3,2,1,0:T(8,128)(2,1)}, u32[]{:S(2)}) copy-start(bf16[2,256,8,128]{3,2,1,0:T(8,128)(2,1)} %param.10) | copy-start | bytes 3145732
  8.2 1.2 %copy-start.2 = (bf16[2,256,8,128]{3,2,1,0:T(8,128)(2,1)S(1)}, bf16[2,256,8,128]{3,2,1,0:T(8,128)(2,1)}, u32[]{:S(2)}) copy-start(bf16[2,256,8,128]{3,2,1,0:T(8,128)(2,1)} %param.15) | copy-start | bytes 3145732
  9.4 0.7 copy-start.3
  14.2 9.5 %collective-permute-start.1 = (bf16[528,256]{1,0:T(8,128)(2,1)S(1)}, bf16[528,256]{1,0:T(8,128)(2,1)S(1)}, u32[]{:S(2)}, u32[]{:S(2)}) collective-permute-start(bf16[528,256]{1,0:T(8,128)(2,1)S(1)} %collective-permute-done.refs_1_.refs_6_), channel_id=1, source_target_pairs={{0,2},{1,3},{2,4},{3,5},{4,6},{5,7},{6,0},{7,1},{8,10},{9,11},{10,... | collective-permute-start | bytes 811016 | tf_op jit(solution)/shard_map/ppermute | solution.py:629
  14.2 14.6 %collective-permute-start.4 = (bf16[528,256]{1,0:T(8,128)(2,1)S(1)}, bf16[528,256]{1,0:T(8,128)(2,1)S(1)}, u32[]{:S(2)}, u32[]{:S(2)}) collective-permute-start(bf16[528,256]{1,0:T(8,128)(2,1)S(1)} %collective-permute-done.refs_1_.refs_6_), channel_id=1, source_target_pairs={{0,1},{1,0},{2,3},{3,2},{4,5},{5,4},{6,7},{7,6},{8,9},{9,8},{10,11... | collective-permute-start | bytes 811016 | tf_op jit(solution)/shard_map/ppermute | solution.py:632
  23.7 11.2 %collective-permute-start.3 = (bf16[528,256]{1,0:T(8,128)(2,1)S(1)}, bf16[528,256]{1,0:T(8,128)(2,1)S(1)}, u32[]{:S(2)}, u32[]{:S(2)}) collective-permute-start(bf16[528,256]{1,0:T(8,128)(2,1)S(1)} %collective-permute-done.1.refs_1_.refs_2_.refs_6_), channel_id=1, source_target_pairs={{0,2},{1,3},{2,4},{3,5},{4,6},{5,7},{6,0},{7,1},{8,10},{9,11},{10,... | collective-permute-start | bytes 811016 | tf_op jit(solution)/shard_map/ppermute | solution.py:629
  23.7 11.2 %collective-permute-start.5 = (bf16[528,256]{1,0:T(8,128)(2,1)S(1)}, bf16[528,256]{1,0:T(8,128)(2,1)S(1)}, u32[]{:S(2)}, u32[]{:S(2)}) collective-permute-start(bf16[528,256]{1,0:T(8,128)(2,1)S(1)} %collective-permute-done.1.refs_1_.refs_2_.refs_6_), channel_id=1, source_target_pairs={{0,1},{1,0},{2,3},{3,2},{4,5},{5,4},{6,7},{7,6},{8,9},{9,8},{10,11... | collective-permute-start | bytes 811016 | tf_op jit(solution)/shard_map/ppermute | solution.py:632
  25.8 11.2 %collective-permute-start.6 = (bf16[528,256]{1,0:T(8,128)(2,1)S(1)}, bf16[528,256]{1,0:T(8,128)(2,1)S(1)}, u32[]{:S(2)}, u32[]{:S(2)}) collective-permute-start(bf16[528,256]{1,0:T(8,128)(2,1)S(1)} %collective-permute-done.2.refs_0_.refs_4_.refs_5_), channel_id=1, source_target_pairs={{0,6},{1,7},{2,0},{3,1},{4,2},{5,3},{6,4},{7,5},{8,14},{9,15},{10,... | collective-permute-start | bytes 811016 | tf_op jit(solution)/shard_map/ppermute | solution.py:629
  42.5 9.3 %collective-permute-start.7 = (bf16[560,256]{1,0:T(8,128)(2,1)S(1)}, bf16[560,256]{1,0:T(8,128)(2,1)S(1)}, u32[]{:S(2)}, u32[]{:S(2)}) collective-permute-start(bf16[560,256]{1,0:T(8,128)(2,1)S(1)} %get-tuple-element.68), channel_id=1, source_target_pairs={{0,1},{1,0},{2,3},{3,2},{4,5},{5,4},{6,7},{7,6},{8,9},{9,8},{10,11... | collective-permute-start | bytes 860168 | tf_op jit(solution)/shard_map/ppermute | solution.py:632
  43.5 8.3 %collective-permute-start.8 = (bf16[528,256]{1,0:T(8,128)(2,1)S(1)}, bf16[528,256]{1,0:T(8,128)(2,1)S(1)}, u32[]{:S(2)}, u32[]{:S(2)}) collective-permute-start(bf16[528,256]{1,0:T(8,128)(2,1)S(1)} %get-tuple-element.69), channel_id=1, source_target_pairs={{0,6},{1,7},{2,0},{3,1},{4,2},{5,3},{6,4},{7,5},{8,14},{9,15},{10,... | collective-permute-start | bytes 811016 | tf_op jit(solution)/shard_map/ppermute | solution.py:629
  43.5 14.3 %collective-permute-start.9 = (bf16[528,256]{1,0:T(8,128)(2,1)S(1)}, bf16[528,256]{1,0:T(8,128)(2,1)S(1)}, u32[]{:S(2)}, u32[]{:S(2)}) collective-permute-start(bf16[528,256]{1,0:T(8,128)(2,1)S(1)} %get-tuple-element.73), channel_id=1, source_target_pairs={{0,2},{1,3},{2,4},{3,5},{4,6},{5,7},{6,0},{7,1},{8,10},{9,11},{10,... | collective-permute-start | bytes 811016 | tf_op jit(solution)/shard_map/ppermute | solution.py:629
  51.9 11.4 %collective-permute-start.11 = (bf16[528,256]{1,0:T(8,128)(2,1)S(1)}, bf16[528,256]{1,0:T(8,128)(2,1)S(1)}, u32[]{:S(2)}, u32[]{:S(2)}) collective-permute-start(bf16[528,256]{1,0:T(8,128)(2,1)S(1)} %get-tuple-element.76), channel_id=1, source_target_pairs={{0,6},{1,7},{2,0},{3,1},{4,2},{5,3},{6,4},{7,5},{8,14},{9,15},{10,... | collective-permute-start | bytes 811016 | tf_op jit(solution)/shard_map/ppermute | solution.py:629
  54.5 8.8 %collective-permute-start.10 = (bf16[512,256]{1,0:T(8,128)(2,1)S(1)}, bf16[512,256]{1,0:T(8,128)(2,1)S(1)}, u32[]{:S(2)}, u32[]{:S(2)}) collective-permute-start(bf16[512,256]{1,0:T(8,128)(2,1)S(1)} %get-tuple-element.75), channel_id=1, source_target_pairs={{0,1},{1,0},{2,3},{3,2},{4,5},{5,4},{6,7},{7,6},{8,9},{9,8},{10,11... | collective-permute-start | bytes 786440 | tf_op jit(solution)/shard_map/ppermute | solution.py:632
  58.3 10.7 %collective-permute-start.12 = (bf16[528,256]{1,0:T(8,128)(2,1)S(1)}, bf16[528,256]{1,0:T(8,128)(2,1)S(1)}, u32[]{:S(2)}, u32[]{:S(2)}) collective-permute-start(bf16[528,256]{1,0:T(8,128)(2,1)S(1)} %get-tuple-element.82), channel_id=1, source_target_pairs={{0,1},{1,0},{2,3},{3,2},{4,5},{5,4},{6,7},{7,6},{8,9},{9,8},{10,11... | collective-permute-start | bytes 811016 | tf_op jit(solution)/shard_map/ppermute | solution.py:632
  63.4 6.5 %collective-permute-start.13 = (bf16[528,256]{1,0:T(8,128)(2,1)S(1)}, bf16[528,256]{1,0:T(8,128)(2,1)S(1)}, u32[]{:S(2)}, u32[]{:S(2)}) collective-permute-start(bf16[528,256]{1,0:T(8,128)(2,1)S(1)} %add_terms1.1), channel_id=1, source_target_pairs={{0,6},{1,7},{2,0},{3,1},{4,2},{5,3},{6,4},{7,5},{8,14},{9,15},{10,... | collective-permute-start | bytes 811016 | tf_op jit(solution)/shard_map/ppermute | solution.py:629
  70.7 1.2 %collective-permute-start.14 = (f32[16,256]{1,0:T(8,128)S(1)}, f32[16,256]{1,0:T(8,128)S(1)}, u32[]{:S(2)}, u32[]{:S(2)}) collective-permute-start(f32[16,256]{1,0:T(8,128)S(1)} %get-tuple-element.86), channel_id=1, source_target_pairs={{0,8},{8,0},{16,24},{24,16},{1,9},{9,1},{17,25},{25,17},{2,10},{10... | collective-permute-start | bytes 49160 | tf_op jit(solution)/shard_map/ppermute | solution.py:695
  71.9 6.3 %collective-permute-start.15 = (f32[16,256]{1,0:T(8,128)S(1)}, f32[16,256]{1,0:T(8,128)S(1)}, u32[]{:S(2)}, u32[]{:S(2)}) collective-permute-start(f32[16,256]{1,0:T(8,128)S(1)} %add.6), channel_id=1, source_target_pairs={{0,16},{8,24},{16,0},{24,8},{1,17},{9,25},{17,1},{25,9},{2,18},{10... | collective-permute-start | bytes 49160 | tf_op jit(solution)/shard_map/ppermute | solution.py:695
where the time goes:
time: 78.5 us; the launch traced here: 78.8 us
  starting transfers between devices  28.7 us (37%)
  waiting for transfers between devices  25.6 us (33%)
  Pallas kernels  20 us (25%)
  local copies, waits for them, and re-layouts  3.75 us (5%)
    ppermute x8, waiting for transfers between devices, hop(): return lax.ppermute(array, 'ctx', pairs)  22.6 us
    ppermute x6, starting transfers between devices, cross(): return lax.ppermute(array, 'ctx', [(c, c ^ 1) for c in range(ctx_size)])  12.9 us
    ppermute x8, starting transfers between devices, hop(): return lax.ppermute(array, 'ctx', pairs)  11.2 us
    pallas_call x5, Pallas kernels, backward_step(): pl.pallas_call(functools.partial(backward_kernel, step, layers, heads, he...  8.88 us
    pallas_call x5, Pallas kernels, forward_step(): pl.pallas_call(functools.partial(forward_kernel, step, layers, heads, hea...  6.21 us
    ppermute x2, starting transfers between devices, per_device(): share = share + lax.ppermute(share, 'resp', pairs)  4.59 us
    unnamed x8, local copies, waits for them, and re-layouts  3.14 us
    ppermute x2, waiting for transfers between devices, per_device(): share = share + lax.ppermute(share, 'resp', pairs)  2.9 us
  transfers between devices with their start and end apart: 16, of which 9 were waited for; matrix products, arithmetic and copies ran while one was open for 0% of the time, Pallas kernels for 15%

commit v1 on v0

--- a/solution.py
+++ b/solution.py
@@ -287,8 +287,6 @@
     if step == layers - 1:
         stay, leave = refs[:2]
         refs = refs[2:]
-    elif step == 1:
-        far, refs = refs[0], refs[1:]
     made = 3 if step == layers else count
     grads, query_out, refs = refs[:made], refs[made], refs[made + 1 :]
     keys, values, turned, probs_held, scores_held, sums = refs
@@ -370,9 +368,6 @@
             rows = pl.ds(edges[part], counts[part])
             own = pl.ds(pl.multiple_of(member * counts[part], counts[part]), counts[part])
             key_part, value_part = sums[rows, :head_dim] * plain, sums[rows, head_dim:]
-            if step == 1 and part == 0:
-                key_part = key_part + far[own, :head_dim].astype(jnp.float32)
-                value_part = value_part + far[own, head_dim:].astype(jnp.float32)
             grads[part][own, :head_dim] = key_part.astype(jnp.bfloat16)
             grads[part][own, head_dim:] = value_part.astype(jnp.bfloat16)
         return carry
@@ -394,34 +389,38 @@
     elif step == layers - 1:
         grads[0][tail:, :] = leave[...]
         grads[1][tail:, :] = stay[leave.shape[0] :, :].astype(jnp.bfloat16)
-    elif step == 1:
-        grads[0][tail:, :] = far[tail:, :]
-
-
-def combine_kernel(step, layers, each, own, side, above, kept, *refs):
+
+
+def combine_kernel(step, layers, each, own, side, above, *refs):
     def wide(ref, rows):
         return ref[rows, :].astype(jnp.float32)
 
     count = own.shape[0]
     rows = slice(0, count)
+    total = wide(own, rows) + wide(side, rows) + wide(above, rows)
+    if step == 0:
+        key_out, value_out = refs
+        total = total.astype(jnp.bfloat16)
+        head_dim = key_out.shape[1]
+        key_out[...] = total[:, :head_dim]
+        value_out[...] = total[:, head_dim:]
+        return
+    kept, *refs = refs
+    if step == 1:
+        crossing, far, *refs = refs
+    out, *refs = refs
     mine = slice(step * each, (step + 1) * each)
     prompt = kept[mine, :] + wide(above, slice(count, None))
     if step == layers - 2:
         prompt = prompt + wide(side, slice(count + mine.start, count + mine.stop))
-    total = wide(own, rows) + wide(side, rows) + wide(above, rows)
-    if step > 0:
-        out = refs[0]
-        out[rows, :] = total.astype(jnp.bfloat16)
-        out[count:, :] = prompt.astype(jnp.bfloat16)
-        if step == layers - 2:
-            refs[1][...] = kept[: step * each, :] + wide(side, slice(count, count + step * each))
-    else:
-        key_out, value_out, prompt_out = refs
-        total = total.astype(jnp.bfloat16)
-        head_dim = key_out.shape[1]
-        key_out[...] = total[:, :head_dim]
-        value_out[...] = total[:, head_dim:]
-        prompt_out[...] = prompt + wide(side, slice(count, None))
+        still_kept, *refs = refs
+        still_kept[...] = kept[: step * each, :] + wide(side, slice(count, count + step * each))
+    out[rows, :] = total.astype(jnp.bfloat16)
+    out[count:, :] = prompt.astype(jnp.bfloat16)
+    if step == 1:
+        (leaving,) = refs
+        leaving[rows, :] = (wide(crossing, rows) + wide(far, rows)).astype(jnp.bfloat16)
+        leaving[count:, :] = far[count:, :]
 
 
 def tile_of(rows):
@@ -493,8 +492,6 @@
         ]
     elif step == layers - 1:
         grad_shapes = [block((layers - 1) * each), block(each)]
-    elif step == 1:
-        grad_shapes = [block(each), block(0)]
     else:
         grad_shapes = [block(0)] * len(counts)
     columns = sum(counts)
@@ -524,19 +521,22 @@
 
 def combine(step, layers, each, *terms):
     count, width = terms[0].shape
-    if step > 0:
-        shapes = [jax.ShapeDtypeStruct((count + each, width), jnp.bfloat16)]
+    message = jax.ShapeDtypeStruct((count + each, width), jnp.bfloat16)
+    if step == 0:
+        shapes = [jax.ShapeDtypeStruct((count, width // 2), jnp.bfloat16)] * 2
+    else:
+        shapes = [message]
         if step == layers - 2:
             shapes.append(jax.ShapeDtypeStruct((step * each, width), jnp.float32))
-    else:
-        shapes = [jax.ShapeDtypeStruct((count, width // 2), jnp.bfloat16)] * 2
-        shapes.append(jax.ShapeDtypeStruct((each, width), jnp.float32))
+        if step == 1:
+            shapes.append(message)
     return pl.pallas_call(
         functools.partial(combine_kernel, step, layers, each),
         in_specs=[WHOLE] * len(terms),
         out_specs=[WHOLE] * len(shapes),
         out_shape=shapes,
         compiler_params=PARAMS,
+        cost_estimate=LITTLE,
         name=f"add_terms{step}",
     )(*terms)
 
@@ -677,23 +677,40 @@
         grads, moved = backward_step(
             step, layers, heads, tokens, each, held_rows, final, messages, moved, terms
         )
-        terms = [far] if step == 2 else []
+        terms = []
         if step == layers:
             far, terms = hop(grads[0], 1 - layers), list(grads[1:])
             kept = grads[1]
         elif step == layers - 1:
             message = grads[1]
         elif step > 0:
-            message, *more = combine(step, layers, each, grads[-1], side, above, kept)
-            kept = more[0] if more else kept
+            crossing = [grads[0], far] if step == 1 else []
+            message, *more = combine(
+                step, layers, each, grads[-1], side, above, kept, *crossing
+            )
+            if step == layers - 2:
+                kept, *more = more
+            if step == 1:
+                grads = more
         if 0 < step < layers:
             side = cross(grads[0])
-    key_grads, value_grads, share = combine(0, layers, each, grads[-1], side, above, kept)
-    stride = 1
-    while stride < resp_size:
-        pairs = [(c, c ^ stride) for c in range(resp_size)]
-        share = share + lax.ppermute(share, "resp", pairs)
-        stride *= 2
+    above, side, last = lax.optimization_barrier((above, side, grads[-1]))
+    share = kept[:each]
+    for term in (above, side):
+        share = share + term[-each:].astype(jnp.float32)
+    key_grads, value_grads = combine(0, layers, each, last, side, above)
+    if resp_size <= 4:
+        shares = [
+            lax.ppermute(share, "resp", [(c, c ^ i) for c in range(resp_size)])
+            for i in range(1, resp_size)
+        ]
+        share = functools.reduce(jnp.add, shares, share)
+    else:
+        stride = 1
+        while stride < resp_size:
+            pairs = [(c, c ^ stride) for c in range(resp_size)]
+            share = share + lax.ppermute(share, "resp", pairs)
+            stride *= 2
     return (
         moved.reshape(queries.shape),
         key_grads.reshape(resp_keys.shape),

time: 78.5 us -> 78.2 us (level); the launches traced: 78.8 us -> 77.3 us
  waiting for transfers between devices: 25.6 us -> 34.6 us
  starting transfers between devices: 28.7 us -> 20.9 us
  Pallas kernels: 20 us -> 17.3 us
    ppermute x6, waiting for transfers between devices: 0.02 us -> 5.44 us  [cross(): return lax.ppermute(array, 'ctx', [(c, c ^ 1) for c in range(ctx_size)])]
    ppermute x8, waiting for transfers between devices: 22.6 us -> 28 us  [hop(): return lax.ppermute(array, 'ctx', pairs)]
    ppermute x6, starting transfers between devices: 12.9 us -> 7.95 us  [cross(): return lax.ppermute(array, 'ctx', [(c, c ^ 1) for c in range(ctx_size)])]
    ppermute x2 -> x3, starting transfers between devices: 4.59 us -> 1.86 us  [per_device(): lax.ppermute(share, 'resp', [(c, c ^ i) for c in range(resp_size)])]
    ppermute x2 -> x3, waiting for transfers between devices: 2.9 us -> 1.18 us  [per_device(): lax.ppermute(share, 'resp', [(c, c ^ i) for c in range(resp_size)])]
    pallas_call x5, Pallas kernels: 8.88 us -> 7.45 us  [backward_step(): pl.pallas_call(functools.partial(backward_kernel, step, layers, heads, he...]
    pallas_call x5, Pallas kernels: 6.21 us -> 5.23 us  [forward_step(): pl.pallas_call(functools.partial(forward_kernel, step, layers, heads, hea...]
  transfers between devices with their start and end apart: 16 -> 17, of which waited for: 9 -> 12; matrix products, arithmetic and copies ran while one was open for 0% -> 0% of each run, Pallas kernels for 15% -> 14%
where the time goes in v1:
time: 78.2 us; the launch traced here: 77.3 us
  waiting for transfers between devices  34.6 us (44%)
  starting transfers between devices  20.9 us (27%)
  Pallas kernels  17.3 us (22%)
  local copies, waits for them, and re-layouts  3.75 us (5%)
  between operations  0.8 us (1%)
    ppermute x8, waiting for transfers between devices, hop(): return lax.ppermute(array, 'ctx', pairs)  28 us
    ppermute x8, starting transfers between devices, hop(): return lax.ppermute(array, 'ctx', pairs)  11.1 us
    ppermute x6, starting transfers between devices, cross(): return lax.ppermute(array, 'ctx', [(c, c ^ 1) for c in range(ctx_size)])  7.95 us
    pallas_call x5, Pallas kernels, backward_step(): pl.pallas_call(functools.partial(backward_kernel, step, layers, heads, he...  7.45 us
    ppermute x6, waiting for transfers between devices, cross(): return lax.ppermute(array, 'ctx', [(c, c ^ 1) for c in range(ctx_size)])  5.44 us
    pallas_call x5, Pallas kernels, forward_step(): pl.pallas_call(functools.partial(forward_kernel, step, layers, heads, hea...  5.23 us
    unnamed x8, local copies, waits for them, and re-layouts  3.14 us
    ppermute x3, starting transfers between devices, per_device(): lax.ppermute(share, 'resp', [(c, c ^ i) for c in range(resp_size)])  1.86 us
  transfers between devices with their start and end apart: 17, of which 12 were waited for; matrix products, arithmetic and copies ran while one was open for 0% of the time, Pallas kernels for 14%

profile of v1, /device:TPU:0, one launch (start us, length us, event | category | flops | bytes accessed | tf_op | source)
XLA Modules:
  0.0 77.3 jit_solution(17876135464443857844)
XLA Ops:
  0.6 1.8 %join_pairs.1 = (bf16[528,256]{1,0:T(8,128)(2,1)}, f32[4,256]{1,0:T(4,128)}) custom-call(bf16[512,128]{1,0:T(8,128)(2,1)} %bitcast.9, bf16[512,128]{1,0:T(8,128)(2,1)} %bitcast.10, bf16[16,128]{1,0:T(8,128)(2,1)} %prompt_keys.1, bf16[16,128]{1,0:T(8,128)(2,1)} %prompt_values.1, f32[2,256]{1,0:T(2,128)} %behaved.1, f32[2,256]{1,0:T(2,128)} %current.1, ...), custom_call_target="tpu_custom_call" | custom-call | flops 1000 | bytes 1000 | tf_op jit(solution)/shard_map/join_pairs/pallas_call | solution.py:588
  2.4 0.0 copy-start
  2.4 3.1 %collective-permute-start = (bf16[528,256]{1,0:T(8,128)(2,1)}, bf16[528,256]{1,0:T(8,128)(2,1)S(1)}, u32[]{:S(2)}, u32[]{:S(2)}) collective-permute-start(bf16[528,256]{1,0:T(8,128)(2,1)} %get-tuple-element.55.refs_0_.refs_5_), channel_id=1, source_target_pairs={{0,2},{1,3},{2,4},{3,5},{4,6},{5,7},{6,0},{7,1},{8,10},{9,11},{10,... | collective-permute-start | bytes 811016 | tf_op jit(solution)/shard_map/ppermute | solution.py:629
  5.5 1.5 %collective-permute-start.2 = (bf16[528,256]{1,0:T(8,128)(2,1)}, bf16[528,256]{1,0:T(8,128)(2,1)S(1)}, u32[]{:S(2)}, u32[]{:S(2)}) collective-permute-start(bf16[528,256]{1,0:T(8,128)(2,1)} %get-tuple-element.55.refs_0_.refs_5_), channel_id=1, source_target_pairs={{0,1},{1,0},{2,3},{3,2},{4,5},{5,4},{6,7},{7,6},{8,9},{9,8},{10,11... | collective-permute-start | bytes 811016 | tf_op jit(solution)/shard_map/ppermute | solution.py:632
  7.0 1.2 %copy-done.1 = bf16[2,256,8,128]{3,2,1,0:T(8,128)(2,1)S(1)} copy-done((bf16[2,256,8,128]{3,2,1,0:T(8,128)(2,1)S(1)}, bf16[2,256,8,128]{3,2,1,0:T(8,128)(2,1)}, u32[]{:S(2)}) %copy-start.1) | copy-done | bytes 1048600
  8.2 1.2 %copy-done.2 = bf16[2,256,8,128]{3,2,1,0:T(8,128)(2,1)S(1)} copy-done((bf16[2,256,8,128]{3,2,1,0:T(8,128)(2,1)S(1)}, bf16[2,256,8,128]{3,2,1,0:T(8,128)(2,1)}, u32[]{:S(2)}) %copy-start.2) | copy-done | bytes 1048600
  9.4 0.7 copy-done.3
  10.1 1.8 %prepare_rows.1 = (f32[2,8,2048]{2,1,0:T(8,128)S(1)}, bf16[2,2048,128]{2,1,0:T(8,128)(2,1)S(1)}, bf16[2,2048,128]{2,1,0:T(8,128)(2,1)S(1)}, bf16[2,128,2048]{2,1,0:T(8,128)(2,1)S(1)}, bf16[2,128,2048]{2,1,0:T(8,128)(2,1)S(1)}) custom-call(f32[4,256]{1,0:T(4,128)S(1)} %copy-done.3, bf16[2,2048,128]{2,1,0:T(8,128)(2,1)S(1)} %bitcast.7, ...), custom_call_target="tpu_custom_call" | custom-call | flops 1000 | bytes 1000 | tf_op jit(solution)/shard_map/prepare_rows/pallas_call | solution.py:441
  11.9 2.3 %collective-permute-done.refs_1_.refs_6_ = bf16[528,256]{1,0:T(8,128)(2,1)S(1)} collective-permute-done((bf16[528,256]{1,0:T(8,128)(2,1)}, bf16[528,256]{1,0:T(8,128)(2,1)S(1)}, u32[]{:S(2)}, u32[]{:S(2)}) %collective-permute-start) | collective-permute-done | bytes 270368 | tf_op jit(solution)/shard_map/ppermute | solution.py:629
  14.2 0.0 collective-permute-start.1
  14.2 1.5 %collective-permute-start.4 = (bf16[528,256]{1,0:T(8,128)(2,1)S(1)}, bf16[528,256]{1,0:T(8,128)(2,1)S(1)}, u32[]{:S(2)}, u32[]{:S(2)}) collective-permute-start(bf16[528,256]{1,0:T(8,128)(2,1)S(1)} %collective-permute-done.refs_1_.refs_6_), channel_id=1, source_target_pairs={{0,1},{1,0},{2,3},{3,2},{4,5},{5,4},{6,7},{7,6},{8,9},{9,8},{10,11... | collective-permute-start | bytes 811016 | tf_op jit(solution)/shard_map/ppermute | solution.py:632
  15.7 2.5 %attend_step0.1.earlier = f32[2,8,2048]{2,1,0:T(8,128)S(1)} custom-call(bf16[2,128,2048]{2,1,0:T(8,128)(2,1)S(1)} %get-tuple-element.53.turned_q.refs_2_, bf16[2,128,2048]{2,1,0:T(8,128)(2,1)S(1)} %get-tuple-element.54.turned_g.refs_3_, f32[2,8,2048]{2,1,0:T(8,128)S(1)} %get-tuple-element.58.earlier, ...), custom_call_target="tpu_custom_call", output_to_operand_aliasing={{}: (2, {})} | custom-call | flops 1000 | bytes 1000 | tf_op jit(solution)/shard_map/attend_step0/pallas_call | solution.py:463
  18.2 0.3 attend_step1.1.earlier
  18.5 5.2 %collective-permute-done.1.refs_1_.refs_2_.refs_6_ = bf16[528,256]{1,0:T(8,128)(2,1)S(1)} collective-permute-done((bf16[528,256]{1,0:T(8,128)(2,1)S(1)}, bf16[528,256]{1,0:T(8,128)(2,1)S(1)}, u32[]{:S(2)}, u32[]{:S(2)}) %collective-permute-start.1) | collective-permute-done | bytes 270368 | tf_op jit(solution)/shard_map/ppermute | solution.py:629
  23.7 1.3 %collective-permute-start.5 = (bf16[528,256]{1,0:T(8,128)(2,1)S(1)}, bf16[528,256]{1,0:T(8,128)(2,1)S(1)}, u32[]{:S(2)}, u32[]{:S(2)}) collective-permute-start(bf16[528,256]{1,0:T(8,128)(2,1)S(1)} %collective-permute-done.1.refs_1_.refs_2_.refs_6_), channel_id=1, source_target_pairs={{0,1},{1,0},{2,3},{3,2},{4,5},{5,4},{6,7},{7,6},{8,9},{9,8},{10,11... | collective-permute-start | bytes 811016 | tf_op jit(solution)/shard_map/ppermute | solution.py:632
  25.0 3.8 %collective-permute-start.6 = (bf16[528,256]{1,0:T(8,128)(2,1)S(1)}, bf16[528,256]{1,0:T(8,128)(2,1)S(1)}, u32[]{:S(2)}, u32[]{:S(2)}) collective-permute-start(bf16[528,256]{1,0:T(8,128)(2,1)S(1)} %collective-permute-done.2.refs_0_.refs_4_.refs_5_), channel_id=1, source_target_pairs={{0,6},{1,7},{2,0},{3,1},{4,2},{5,3},{6,4},{7,5},{8,14},{9,15},{10,... | collective-permute-start | bytes 811016 | tf_op jit(solution)/shard_map/ppermute | solution.py:629
  28.8 0.3 attend_step2.1.earlier
  29.1 5.8 %collective-permute-done.3.refs_1_.refs_3_.refs_6_ = bf16[528,256]{1,0:T(8,128)(2,1)S(1)} collective-permute-done((bf16[528,256]{1,0:T(8,128)(2,1)S(1)}, bf16[528,256]{1,0:T(8,128)(2,1)S(1)}, u32[]{:S(2)}, u32[]{:S(2)}) %collective-permute-start.3) | collective-permute-done | bytes 270368 | tf_op jit(solution)/shard_map/ppermute | solution.py:629
  34.9 0.3 attend_step3.1.earlier
  35.2 1.8 %collective-permute-done.6.refs_7_.refs_5_ = bf16[528,256]{1,0:T(8,128)(2,1)S(1)} collective-permute-done((bf16[528,256]{1,0:T(8,128)(2,1)S(1)}, bf16[528,256]{1,0:T(8,128)(2,1)S(1)}, u32[]{:S(2)}, u32[]{:S(2)}) %collective-permute-start.6) | collective-permute-done | bytes 270368 | tf_op jit(solution)/shard_map/ppermute | solution.py:629
  37.0 1.9 %attend_step4.1 = (f32[2,8,2048]{2,1,0:T(8,128)S(1)}, bf16[128,256]{1,0:T(8,128)(2,1)S(1)}) custom-call(bf16[2,128,2048]{2,1,0:T(8,128)(2,1)S(1)} %get-tuple-element.53.turned_q.refs_2_, bf16[2,128,2048]{2,1,0:T(8,128)(2,1)S(1)} %get-tuple-element.54.turned_g.refs_3_, f32[2,8,2048]{2,1,0:T(8,128)S(1)} %attend_step3.1.earlier, ...), custom_call_target="tpu_custom_call", output_to_operand_aliasing={{0}: (2, {})} | custom-call | flops 1000 | bytes 1000 | tf_op jit(solution)/shard_map/attend_step4/pallas_call | solution.py:463
  38.9 2.2 %attend_grad_step4.1 = (bf16[528,256]{1,0:T(8,128)(2,1)S(1)}, f32[64,256]{1,0:T(8,128)S(1)}, bf16[48,256]{1,0:T(8,128)(2,1)S(1)}, f32[2,128,2048]{2,1,0:T(8,128)S(1)}) custom-call(bf16[2,2048,128]{2,1,0:T(8,128)(2,1)S(1)} %get-tuple-element.51.refs_0_, bf16[2,2048,128]{2,1,0:T(8,128)(2,1)S(1)} %get-tuple-element.52.refs_1_, ...), custom_call_target="tpu_custom_call" | custom-call | flops 1000 | bytes 1000 | tf_op jit(solution)/shard_map/attend_grad_step4/pallas_call | solution.py:505
  41.2 0.4 attend_grad_step3.1
  41.5 0.1 collective-permute-start.7
  41.6 0.1 collective-permute-start.8
  41.7 2.0 %collective-permute-start.11 = (bf16[528,256]{1,0:T(8,128)(2,1)S(1)}, bf16[528,256]{1,0:T(8,128)(2,1)S(1)}, u32[]{:S(2)}, u32[]{:S(2)}) collective-permute-start(bf16[528,256]{1,0:T(8,128)(2,1)S(1)} %get-tuple-element.82), channel_id=1, source_target_pairs={{0,2},{1,3},{2,4},{3,5},{4,6},{5,7},{6,0},{7,1},{8,10},{9,11},{10,... | collective-permute-start | bytes 811016 | tf_op jit(solution)/shard_map/ppermute | solution.py:629
  43.7 0.3 attend_grad_step2.1
  44.1 5.8 %collective-permute-done.8.above = bf16[528,256]{1,0:T(8,128)(2,1)S(1)} collective-permute-done((bf16[528,256]{1,0:T(8,128)(2,1)S(1)}, bf16[528,256]{1,0:T(8,128)(2,1)S(1)}, u32[]{:S(2)}, u32[]{:S(2)}) %collective-permute-start.8) | collective-permute-done | bytes 270368 | tf_op jit(solution)/shard_map/ppermute | solution.py:629
  49.8 0.3 collective-permute-done.7.side
  50.1 0.1 add_terms2.1
  50.2 2.0 %collective-permute-start.10 = (bf16[528,256]{1,0:T(8,128)(2,1)S(1)}, bf16[528,256]{1,0:T(8,128)(2,1)S(1)}, u32[]{:S(2)}, u32[]{:S(2)}) collective-permute-start(bf16[528,256]{1,0:T(8,128)(2,1)S(1)} %get-tuple-element.79), channel_id=1, source_target_pairs={{0,6},{1,7},{2,0},{3,1},{4,2},{5,3},{6,4},{7,5},{8,14},{9,15},{10,... | collective-permute-start | bytes 811016 | tf_op jit(solution)/shard_map/ppermute | solution.py:629
  52.3 2.0 %collective-permute-start.9 = (bf16[512,256]{1,0:T(8,128)(2,1)S(1)}, bf16[512,256]{1,0:T(8,128)(2,1)S(1)}, u32[]{:S(2)}, u32[]{:S(2)}) collective-permute-start(bf16[512,256]{1,0:T(8,128)(2,1)S(1)} %get-tuple-element.78), channel_id=1, source_target_pairs={{0,1},{1,0},{2,3},{3,2},{4,5},{5,4},{6,7},{7,6},{8,9},{9,8},{10,11... | collective-permute-start | bytes 786440 | tf_op jit(solution)/shard_map/ppermute | solution.py:632
  54.2 0.3 attend_grad_step1.1
  54.6 4.8 %collective-permute-done.9.side = bf16[512,256]{1,0:T(8,128)(2,1)S(1)} collective-permute-done((bf16[512,256]{1,0:T(8,128)(2,1)S(1)}, bf16[512,256]{1,0:T(8,128)(2,1)S(1)}, u32[]{:S(2)}, u32[]{:S(2)}) %collective-permute-start.9) | collective-permute-done | bytes 262176 | tf_op jit(solution)/shard_map/ppermute | solution.py:632
  59.4 4.4 %collective-permute-done.10.above = bf16[528,256]{1,0:T(8,128)(2,1)S(1)} collective-permute-done((bf16[528,256]{1,0:T(8,128)(2,1)S(1)}, bf16[528,256]{1,0:T(8,128)(2,1)S(1)}, u32[]{:S(2)}, u32[]{:S(2)}) %collective-permute-start.10) | collective-permute-done | bytes 270368 | tf_op jit(solution)/shard_map/ppermute | solution.py:629
  63.8 0.2 add_terms1.1
  64.0 0.1 collective-permute-start.12
  64.1 1.6 %collective-permute-start.13 = (bf16[528,256]{1,0:T(8,128)(2,1)S(1)}, bf16[528,256]{1,0:T(8,128)(2,1)S(1)}, u32[]{:S(2)}, u32[]{:S(2)}) collective-permute-start(bf16[528,256]{1,0:T(8,128)(2,1)S(1)} %get-tuple-element.88), channel_id=1, source_target_pairs={{0,1},{1,0},{2,3},{3,2},{4,5},{5,4},{6,7},{7,6},{8,9},{9,8},{10,11... | collective-permute-start | bytes 811016 | tf_op jit(solution)/shard_map/ppermute | solution.py:632
  65.7 4.2 %attend_grad_step0.1 = (bf16[512,256]{1,0:T(8,128)(2,1)S(1)}, bf16[2,2048,128]{2,1,0:T(8,128)(2,1)}) custom-call(bf16[2,2048,128]{2,1,0:T(8,128)(2,1)S(1)} %get-tuple-element.51.refs_0_, bf16[2,2048,128]{2,1,0:T(8,128)(2,1)S(1)} %get-tuple-element.52.refs_1_, bf16[2,128,2048]{2,1,0:T(8,128)(2,1)S(1)} %get-tuple-element.53.turned_q.refs_2_, ...), custom_call_target="tpu_custom_call" | custom-call | flops 1000 | bytes 1000 | tf_op jit(solution)/shard_map/attend_grad_step0/pallas_call | solution.py:505
  69.8 2.7 %collective-permute-done.12.above = bf16[528,256]{1,0:T(8,128)(2,1)S(1)} collective-permute-done((bf16[528,256]{1,0:T(8,128)(2,1)S(1)}, bf16[528,256]{1,0:T(8,128)(2,1)S(1)}, u32[]{:S(2)}, u32[]{:S(2)}) %collective-permute-start.12) | collective-permute-done | bytes 270368 | tf_op jit(solution)/shard_map/ppermute | solution.py:629
  72.5 0.3 collective-permute-done.13.side
  72.9 1.2 %collective-permute-start.15 = (f32[16,256]{1,0:T(8,128)S(1)}, f32[16,256]{1,0:T(8,128)S(1)}, u32[]{:S(2)}, u32[]{:S(2)}) collective-permute-start(f32[16,256]{1,0:T(8,128)S(1)} %convert_add_fusion), channel_id=1, source_target_pairs={{0,16},{8,24},{16,0},{24,8},{1,17},{9,25},{17,1},{25,9},{2,18},{10... | collective-permute-start | bytes 49160 | tf_op jit(solution)/shard_map/ppermute | solution.py:704
  74.1 0.7 collective-permute-start.14
  74.8 0.8 add_terms0.1
  75.5 0.5 collective-permute-done.16
  76.1 0.6 collective-permute-done.15
  76.7 0.0 collective-permute-done.14
  76.7 0.6 fusion
  (12 shorter events, 0.0 us)
Async XLA Ops:
  2.4 13.3 %copy-start = (bf16[528,256]{1,0:T(8,128)(2,1)S(1)}, bf16[528,256]{1,0:T(8,128)(2,1)}, u32[]{:S(2)}) copy-start(bf16[528,256]{1,0:T(8,128)(2,1)} %get-tuple-element.55.refs_0_.refs_5_) | copy-start | bytes 811012
  2.4 11.8 %collective-permute-start = (bf16[528,256]{1,0:T(8,128)(2,1)}, bf16[528,256]{1,0:T(8,128)(2,1)S(1)}, u32[]{:S(2)}, u32[]{:S(2)}) collective-permute-start(bf16[528,256]{1,0:T(8,128)(2,1)} %get-tuple-element.55.refs_0_.refs_5_), channel_id=1, source_target_pairs={{0,2},{1,3},{2,4},{3,5},{4,6},{5,7},{6,0},{7,1},{8,10},{9,11},{10,... | collective-permute-start | bytes 811016 | tf_op jit(solution)/shard_map/ppermute | solution.py:629
  5.5 12.7 %collective-permute-start.2 = (bf16[528,256]{1,0:T(8,128)(2,1)}, bf16[528,256]{1,0:T(8,128)(2,1)S(1)}, u32[]{:S(2)}, u32[]{:S(2)}) collective-permute-start(bf16[528,256]{1,0:T(8,128)(2,1)} %get-tuple-element.55.refs_0_.refs_5_), channel_id=1, source_target_pairs={{0,1},{1,0},{2,3},{3,2},{4,5},{5,4},{6,7},{7,6},{8,9},{9,8},{10,11... | collective-permute-start | bytes 811016 | tf_op jit(solution)/shard_map/ppermute | solution.py:632
  7.0 1.2 %copy-start.1 = (bf16[2,256,8,128]{3,2,1,0:T(8,128)(2,1)S(1)}, bf16[2,256,8,128]{3,2,1,0:T(8,128)(2,1)}, u32[]{:S(2)}) copy-start(bf16[2,256,8,128]{3,2,1,0:T(8,128)(2,1)} %param.10) | copy-start | bytes 3145732
  8.2 1.2 %copy-start.2 = (bf16[2,256,8,128]{3,2,1,0:T(8,128)(2,1)S(1)}, bf16[2,256,8,128]{3,2,1,0:T(8,128)(2,1)}, u32[]{:S(2)}) copy-start(bf16[2,256,8,128]{3,2,1,0:T(8,128)(2,1)} %param.15) | copy-start | bytes 3145732
  9.4 0.7 copy-start.3
  14.2 9.5 %collective-permute-start.1 = (bf16[528,256]{1,0:T(8,128)(2,1)S(1)}, bf16[528,256]{1,0:T(8,128)(2,1)S(1)}, u32[]{:S(2)}, u32[]{:S(2)}) collective-permute-start(bf16[528,256]{1,0:T(8,128)(2,1)S(1)} %collective-permute-done.refs_1_.refs_6_), channel_id=1, source_target_pairs={{0,2},{1,3},{2,4},{3,5},{4,6},{5,7},{6,0},{7,1},{8,10},{9,11},{10,... | collective-permute-start | bytes 811016 | tf_op jit(solution)/shard_map/ppermute | solution.py:629
  14.2 14.6 %collective-permute-start.4 = (bf16[528,256]{1,0:T(8,128)(2,1)S(1)}, bf16[528,256]{1,0:T(8,128)(2,1)S(1)}, u32[]{:S(2)}, u32[]{:S(2)}) collective-permute-start(bf16[528,256]{1,0:T(8,128)(2,1)S(1)} %collective-permute-done.refs_1_.refs_6_), channel_id=1, source_target_pairs={{0,1},{1,0},{2,3},{3,2},{4,5},{5,4},{6,7},{7,6},{8,9},{9,8},{10,11... | collective-permute-start | bytes 811016 | tf_op jit(solution)/shard_map/ppermute | solution.py:632
  23.7 11.2 %collective-permute-start.3 = (bf16[528,256]{1,0:T(8,128)(2,1)S(1)}, bf16[528,256]{1,0:T(8,128)(2,1)S(1)}, u32[]{:S(2)}, u32[]{:S(2)}) collective-permute-start(bf16[528,256]{1,0:T(8,128)(2,1)S(1)} %collective-permute-done.1.refs_1_.refs_2_.refs_6_), channel_id=1, source_target_pairs={{0,2},{1,3},{2,4},{3,5},{4,6},{5,7},{6,0},{7,1},{8,10},{9,11},{10,... | collective-permute-start | bytes 811016 | tf_op jit(solution)/shard_map/ppermute | solution.py:629
  23.7 11.2 %collective-permute-start.5 = (bf16[528,256]{1,0:T(8,128)(2,1)S(1)}, bf16[528,256]{1,0:T(8,128)(2,1)S(1)}, u32[]{:S(2)}, u32[]{:S(2)}) collective-permute-start(bf16[528,256]{1,0:T(8,128)(2,1)S(1)} %collective-permute-done.1.refs_1_.refs_2_.refs_6_), channel_id=1, source_target_pairs={{0,1},{1,0},{2,3},{3,2},{4,5},{5,4},{6,7},{7,6},{8,9},{9,8},{10,11... | collective-permute-start | bytes 811016 | tf_op jit(solution)/shard_map/ppermute | solution.py:632
  25.0 12.0 %collective-permute-start.6 = (bf16[528,256]{1,0:T(8,128)(2,1)S(1)}, bf16[528,256]{1,0:T(8,128)(2,1)S(1)}, u32[]{:S(2)}, u32[]{:S(2)}) collective-permute-start(bf16[528,256]{1,0:T(8,128)(2,1)S(1)} %collective-permute-done.2.refs_0_.refs_4_.refs_5_), channel_id=1, source_target_pairs={{0,6},{1,7},{2,0},{3,1},{4,2},{5,3},{6,4},{7,5},{8,14},{9,15},{10,... | collective-permute-start | bytes 811016 | tf_op jit(solution)/shard_map/ppermute | solution.py:629
  41.5 8.6 %collective-permute-start.7 = (bf16[560,256]{1,0:T(8,128)(2,1)S(1)}, bf16[560,256]{1,0:T(8,128)(2,1)S(1)}, u32[]{:S(2)}, u32[]{:S(2)}) collective-permute-start(bf16[560,256]{1,0:T(8,128)(2,1)S(1)} %get-tuple-element.72), channel_id=1, source_target_pairs={{0,1},{1,0},{2,3},{3,2},{4,5},{5,4},{6,7},{7,6},{8,9},{9,8},{10,11... | collective-permute-start | bytes 860168 | tf_op jit(solution)/shard_map/ppermute | solution.py:632
  41.6 8.2 %collective-permute-start.8 = (bf16[528,256]{1,0:T(8,128)(2,1)S(1)}, bf16[528,256]{1,0:T(8,128)(2,1)S(1)}, u32[]{:S(2)}, u32[]{:S(2)}) collective-permute-start(bf16[528,256]{1,0:T(8,128)(2,1)S(1)} %get-tuple-element.73), channel_id=1, source_target_pairs={{0,6},{1,7},{2,0},{3,1},{4,2},{5,3},{6,4},{7,5},{8,14},{9,15},{10,... | collective-permute-start | bytes 811016 | tf_op jit(solution)/shard_map/ppermute | solution.py:629
  41.7 17.7 %collective-permute-start.11 = (bf16[528,256]{1,0:T(8,128)(2,1)S(1)}, bf16[528,256]{1,0:T(8,128)(2,1)S(1)}, u32[]{:S(2)}, u32[]{:S(2)}) collective-permute-start(bf16[528,256]{1,0:T(8,128)(2,1)S(1)} %get-tuple-element.82), channel_id=1, source_target_pairs={{0,2},{1,3},{2,4},{3,5},{4,6},{5,7},{6,0},{7,1},{8,10},{9,11},{10,... | collective-permute-start | bytes 811016 | tf_op jit(solution)/shard_map/ppermute | solution.py:629
  50.2 13.6 %collective-permute-start.10 = (bf16[528,256]{1,0:T(8,128)(2,1)S(1)}, bf16[528,256]{1,0:T(8,128)(2,1)S(1)}, u32[]{:S(2)}, u32[]{:S(2)}) collective-permute-start(bf16[528,256]{1,0:T(8,128)(2,1)S(1)} %get-tuple-element.79), channel_id=1, source_target_pairs={{0,6},{1,7},{2,0},{3,1},{4,2},{5,3},{6,4},{7,5},{8,14},{9,15},{10,... | collective-permute-start | bytes 811016 | tf_op jit(solution)/shard_map/ppermute | solution.py:629
  52.3 7.2 %collective-permute-start.9 = (bf16[512,256]{1,0:T(8,128)(2,1)S(1)}, bf16[512,256]{1,0:T(8,128)(2,1)S(1)}, u32[]{:S(2)}, u32[]{:S(2)}) collective-permute-start(bf16[512,256]{1,0:T(8,128)(2,1)S(1)} %get-tuple-element.78), channel_id=1, source_target_pairs={{0,1},{1,0},{2,3},{3,2},{4,5},{5,4},{6,7},{7,6},{8,9},{9,8},{10,11... | collective-permute-start | bytes 786440 | tf_op jit(solution)/shard_map/ppermute | solution.py:632
  64.0 8.6 %collective-permute-start.12 = (bf16[528,256]{1,0:T(8,128)(2,1)S(1)}, bf16[528,256]{1,0:T(8,128)(2,1)S(1)}, u32[]{:S(2)}, u32[]{:S(2)}) collective-permute-start(bf16[528,256]{1,0:T(8,128)(2,1)S(1)} %get-tuple-element.87), channel_id=1, source_target_pairs={{0,6},{1,7},{2,0},{3,1},{4,2},{5,3},{6,4},{7,5},{8,14},{9,15},{10,... | collective-permute-start | bytes 811016 | tf_op jit(solution)/shard_map/ppermute | solution.py:629
  64.1 8.8 %collective-permute-start.13 = (bf16[528,256]{1,0:T(8,128)(2,1)S(1)}, bf16[528,256]{1,0:T(8,128)(2,1)S(1)}, u32[]{:S(2)}, u32[]{:S(2)}) collective-permute-start(bf16[528,256]{1,0:T(8,128)(2,1)S(1)} %get-tuple-element.88), channel_id=1, source_target_pairs={{0,1},{1,0},{2,3},{3,2},{4,5},{5,4},{6,7},{7,6},{8,9},{9,8},{10,11... | collective-permute-start | bytes 811016 | tf_op jit(solution)/shard_map/ppermute | solution.py:632
  72.9 3.2 %collective-permute-start.16 = (f32[16,256]{1,0:T(8,128)S(1)}, f32[16,256]{1,0:T(8,128)S(1)}, u32[]{:S(2)}, u32[]{:S(2)}) collective-permute-start(f32[16,256]{1,0:T(8,128)S(1)} %convert_add_fusion), channel_id=1, source_target_pairs={{0,24},{8,16},{16,8},{24,0},{1,25},{9,17},{17,9},{25,1},{2,26},{10... | collective-permute-start | bytes 49160 | tf_op jit(solution)/shard_map/ppermute | solution.py:704
  72.9 3.8 %collective-permute-start.15 = (f32[16,256]{1,0:T(8,128)S(1)}, f32[16,256]{1,0:T(8,128)S(1)}, u32[]{:S(2)}, u32[]{:S(2)}) collective-permute-start(f32[16,256]{1,0:T(8,128)S(1)} %convert_add_fusion), channel_id=1, source_target_pairs={{0,16},{8,24},{16,0},{24,8},{1,17},{9,25},{17,1},{25,9},{2,18},{10... | collective-permute-start | bytes 49160 | tf_op jit(solution)/shard_map/ppermute | solution.py:704
  74.1 2.6 %collective-permute-start.14 = (f32[16,256]{1,0:T(8,128)S(1)}, f32[16,256]{1,0:T(8,128)S(1)}, u32[]{:S(2)}, u32[]{:S(2)}) collective-permute-start(f32[16,256]{1,0:T(8,128)S(1)} %convert_add_fusion), channel_id=1, source_target_pairs={{0,8},{8,0},{16,24},{24,16},{1,9},{9,1},{17,25},{25,17},{2,10},{10... | collective-permute-start | bytes 49160 | tf_op jit(solution)/shard_map/ppermute | solution.py:704

commit v2 on v1

--- a/solution.py
+++ b/solution.py
@@ -700,23 +700,22 @@
         share = share + term[-each:].astype(jnp.float32)
     key_grads, value_grads = combine(0, layers, each, last, side, above)
     if resp_size <= 4:
-        shares = [
+        shares = [share] + [
             lax.ppermute(share, "resp", [(c, c ^ i) for c in range(resp_size)])
             for i in range(1, resp_size)
         ]
-        share = functools.reduce(jnp.add, shares, share)
     else:
-        stride = 1
+        shares, stride = [share], 1
         while stride < resp_size:
             pairs = [(c, c ^ stride) for c in range(resp_size)]
-            share = share + lax.ppermute(share, "resp", pairs)
+            shares = [sum(shares), lax.ppermute(sum(shares), "resp", pairs)]
             stride *= 2
     return (
         moved.reshape(queries.shape),
         key_grads.reshape(resp_keys.shape),
         value_grads.reshape(resp_values.shape),
-        share[:, :head_dim],
-        share[:, head_dim:],
+        sum(part[:, :head_dim] for part in shares),
+        sum(part[:, head_dim:] for part in shares),
     )
 
 

time: 78.2 us -> 78.1 us (level)
  waiting for transfers between devices: 34.6 us -> 30.7 us
  Pallas kernels: 17.3 us -> 20.1 us
    ppermute x8, waiting for transfers between devices: 28 us -> 24.6 us  [hop(): return lax.ppermute(array, 'ctx', pairs)]
    pallas_call x5, Pallas kernels: 7.45 us -> 8.85 us  [backward_step(): pl.pallas_call(functools.partial(backward_kernel, step, layers, heads, he...]
    pallas_call x5, Pallas kernels: 5.23 us -> 6.24 us  [forward_step(): pl.pallas_call(functools.partial(forward_kernel, step, layers, heads, hea...]
  transfers between devices with their start and end apart: 17 -> 17, of which waited for: 12 -> 10; matrix products, arithmetic and copies ran while one was open for 0% -> 0% of each run, Pallas kernels for 14% -> 17%
where the time goes in v2:
time: 78.1 us; the launch traced here: 76.9 us
  waiting for transfers between devices  30.7 us (39%)
  starting transfers between devices  21.5 us (28%)
  Pallas kernels  20.1 us (26%)
  local copies, waits for them, and re-layouts  3.14 us (4%)
    ppermute x8, waiting for transfers between devices, hop(): return lax.ppermute(array, 'ctx', pairs)  24.6 us
    ppermute x8, starting transfers between devices, hop(): return lax.ppermute(array, 'ctx', pairs)  10.8 us
    pallas_call x5, Pallas kernels, backward_step(): pl.pallas_call(functools.partial(backward_kernel, step, layers, heads, he...  8.85 us
    ppermute x6, starting transfers between devices, cross(): return lax.ppermute(array, 'ctx', [(c, c ^ 1) for c in range(ctx_size)])  8.33 us
    pallas_call x5, Pallas kernels, forward_step(): pl.pallas_call(functools.partial(forward_kernel, step, layers, heads, hea...  6.24 us
    ppermute x6, waiting for transfers between devices, cross(): return lax.ppermute(array, 'ctx', [(c, c ^ 1) for c in range(ctx_size)])  4.99 us
    unnamed x8, local copies, waits for them, and re-layouts  3.14 us
    ppermute x3, starting transfers between devices, per_device(): lax.ppermute(share, 'resp', [(c, c ^ i) for c in range(resp_size)])  2.34 us
  transfers between devices with their start and end apart: 17, of which 10 were waited for; matrix products, arithmetic and copies ran while one was open for 0% of the time, Pallas kernels for 17%

profile of v2, /device:TPU:0, one launch (start us, length us, event | category | flops | bytes accessed | tf_op | source)
XLA Modules:
  0.0 76.9 jit_solution(13908184610288322957)
XLA Ops:
  0.6 1.8 %join_pairs.1 = (bf16[528,256]{1,0:T(8,128)(2,1)}, f32[4,256]{1,0:T(4,128)}) custom-call(bf16[512,128]{1,0:T(8,128)(2,1)} %bitcast.9, bf16[512,128]{1,0:T(8,128)(2,1)} %bitcast.10, bf16[16,128]{1,0:T(8,128)(2,1)} %prompt_keys.1, bf16[16,128]{1,0:T(8,128)(2,1)} %prompt_values.1, f32[2,256]{1,0:T(2,128)} %behaved.1, f32[2,256]{1,0:T(2,128)} %current.1, ...), custom_call_target="tpu_custom_call" | custom-call | flops 1000 | bytes 1000 | tf_op jit(solution)/shard_map/join_pairs/pallas_call | solution.py:588
  2.4 0.0 copy-start
  2.4 3.1 %collective-permute-start = (bf16[528,256]{1,0:T(8,128)(2,1)}, bf16[528,256]{1,0:T(8,128)(2,1)S(1)}, u32[]{:S(2)}, u32[]{:S(2)}) collective-permute-start(bf16[528,256]{1,0:T(8,128)(2,1)} %get-tuple-element.55.refs_0_.refs_5_), channel_id=1, source_target_pairs={{0,2},{1,3},{2,4},{3,5},{4,6},{5,7},{6,0},{7,1},{8,10},{9,11},{10,... | collective-permute-start | bytes 811016 | tf_op jit(solution)/shard_map/ppermute | solution.py:629
  5.5 1.5 %collective-permute-start.2 = (bf16[528,256]{1,0:T(8,128)(2,1)}, bf16[528,256]{1,0:T(8,128)(2,1)S(1)}, u32[]{:S(2)}, u32[]{:S(2)}) collective-permute-start(bf16[528,256]{1,0:T(8,128)(2,1)} %get-tuple-element.55.refs_0_.refs_5_), channel_id=1, source_target_pairs={{0,1},{1,0},{2,3},{3,2},{4,5},{5,4},{6,7},{7,6},{8,9},{9,8},{10,11... | collective-permute-start | bytes 811016 | tf_op jit(solution)/shard_map/ppermute | solution.py:632
  7.0 1.2 %copy-done.1 = bf16[2,256,8,128]{3,2,1,0:T(8,128)(2,1)S(1)} copy-done((bf16[2,256,8,128]{3,2,1,0:T(8,128)(2,1)S(1)}, bf16[2,256,8,128]{3,2,1,0:T(8,128)(2,1)}, u32[]{:S(2)}) %copy-start.1) | copy-done | bytes 1048600
  8.2 1.2 %copy-done.2 = bf16[2,256,8,128]{3,2,1,0:T(8,128)(2,1)S(1)} copy-done((bf16[2,256,8,128]{3,2,1,0:T(8,128)(2,1)S(1)}, bf16[2,256,8,128]{3,2,1,0:T(8,128)(2,1)}, u32[]{:S(2)}) %copy-start.2) | copy-done | bytes 1048600
  9.4 0.7 copy-done.3
  10.1 2.2 %prepare_rows.1 = (f32[2,8,2048]{2,1,0:T(8,128)S(1)}, bf16[2,2048,128]{2,1,0:T(8,128)(2,1)S(1)}, bf16[2,2048,128]{2,1,0:T(8,128)(2,1)S(1)}, bf16[2,128,2048]{2,1,0:T(8,128)(2,1)S(1)}, bf16[2,128,2048]{2,1,0:T(8,128)(2,1)S(1)}) custom-call(f32[4,256]{1,0:T(4,128)S(1)} %copy-done.3, bf16[2,2048,128]{2,1,0:T(8,128)(2,1)S(1)} %bitcast.7, ...), custom_call_target="tpu_custom_call" | custom-call | flops 1000 | bytes 1000 | tf_op jit(solution)/shard_map/prepare_rows/pallas_call | solution.py:441
  12.4 1.8 %collective-permute-done.refs_1_.refs_6_ = bf16[528,256]{1,0:T(8,128)(2,1)S(1)} collective-permute-done((bf16[528,256]{1,0:T(8,128)(2,1)}, bf16[528,256]{1,0:T(8,128)(2,1)S(1)}, u32[]{:S(2)}, u32[]{:S(2)}) %collective-permute-start) | collective-permute-done | bytes 270368 | tf_op jit(solution)/shard_map/ppermute | solution.py:629
  14.2 1.5 %collective-permute-start.4 = (bf16[528,256]{1,0:T(8,128)(2,1)S(1)}, bf16[528,256]{1,0:T(8,128)(2,1)S(1)}, u32[]{:S(2)}, u32[]{:S(2)}) collective-permute-start(bf16[528,256]{1,0:T(8,128)(2,1)S(1)} %collective-permute-done.refs_1_.refs_6_), channel_id=1, source_target_pairs={{0,1},{1,0},{2,3},{3,2},{4,5},{5,4},{6,7},{7,6},{8,9},{9,8},{10,11... | collective-permute-start | bytes 811016 | tf_op jit(solution)/shard_map/ppermute | solution.py:632
  15.7 3.1 %attend_step0.1.earlier = f32[2,8,2048]{2,1,0:T(8,128)S(1)} custom-call(bf16[2,128,2048]{2,1,0:T(8,128)(2,1)S(1)} %get-tuple-element.53.turned_q.refs_2_, bf16[2,128,2048]{2,1,0:T(8,128)(2,1)S(1)} %get-tuple-element.54.turned_g.refs_3_, f32[2,8,2048]{2,1,0:T(8,128)S(1)} %get-tuple-element.58.earlier, ...), custom_call_target="tpu_custom_call", output_to_operand_aliasing={{}: (2, {})} | custom-call | flops 1000 | bytes 1000 | tf_op jit(solution)/shard_map/attend_step0/pallas_call | solution.py:463
  18.8 0.0 collective-permute-done.2.refs_0_.refs_4_.refs_5_
  18.8 0.3 attend_step1.1.earlier
  19.1 4.6 %collective-permute-done.1.refs_1_.refs_2_.refs_6_ = bf16[528,256]{1,0:T(8,128)(2,1)S(1)} collective-permute-done((bf16[528,256]{1,0:T(8,128)(2,1)S(1)}, bf16[528,256]{1,0:T(8,128)(2,1)S(1)}, u32[]{:S(2)}, u32[]{:S(2)}) %collective-permute-start.1) | collective-permute-done | bytes 270368 | tf_op jit(solution)/shard_map/ppermute | solution.py:629
  23.7 0.0 collective-permute-start.3
  23.7 1.3 %collective-permute-start.5 = (bf16[528,256]{1,0:T(8,128)(2,1)S(1)}, bf16[528,256]{1,0:T(8,128)(2,1)S(1)}, u32[]{:S(2)}, u32[]{:S(2)}) collective-permute-start(bf16[528,256]{1,0:T(8,128)(2,1)S(1)} %collective-permute-done.1.refs_1_.refs_2_.refs_6_), channel_id=1, source_target_pairs={{0,1},{1,0},{2,3},{3,2},{4,5},{5,4},{6,7},{7,6},{8,9},{9,8},{10,11... | collective-permute-start | bytes 811016 | tf_op jit(solution)/shard_map/ppermute | solution.py:632
  25.0 3.8 %collective-permute-start.6 = (bf16[528,256]{1,0:T(8,128)(2,1)S(1)}, bf16[528,256]{1,0:T(8,128)(2,1)S(1)}, u32[]{:S(2)}, u32[]{:S(2)}) collective-permute-start(bf16[528,256]{1,0:T(8,128)(2,1)S(1)} %collective-permute-done.2.refs_0_.refs_4_.refs_5_), channel_id=1, source_target_pairs={{0,6},{1,7},{2,0},{3,1},{4,2},{5,3},{6,4},{7,5},{8,14},{9,15},{10,... | collective-permute-start | bytes 811016 | tf_op jit(solution)/shard_map/ppermute | solution.py:629
  28.8 0.0 collective-permute-done.4.refs_0_.refs_5_
  28.8 0.3 attend_step2.1.earlier
  29.0 5.9 %collective-permute-done.3.refs_1_.refs_3_.refs_6_ = bf16[528,256]{1,0:T(8,128)(2,1)S(1)} collective-permute-done((bf16[528,256]{1,0:T(8,128)(2,1)S(1)}, bf16[528,256]{1,0:T(8,128)(2,1)S(1)}, u32[]{:S(2)}, u32[]{:S(2)}) %collective-permute-start.3) | collective-permute-done | bytes 270368 | tf_op jit(solution)/shard_map/ppermute | solution.py:629
  34.9 0.0 collective-permute-done.5.refs_0_.refs_6_.refs_5_
  34.9 0.3 attend_step3.1.earlier
  35.2 1.8 %collective-permute-done.6.refs_7_.refs_5_ = bf16[528,256]{1,0:T(8,128)(2,1)S(1)} collective-permute-done((bf16[528,256]{1,0:T(8,128)(2,1)S(1)}, bf16[528,256]{1,0:T(8,128)(2,1)S(1)}, u32[]{:S(2)}, u32[]{:S(2)}) %collective-permute-start.6) | collective-permute-done | bytes 270368 | tf_op jit(solution)/shard_map/ppermute | solution.py:629
  37.0 2.4 %attend_step4.1 = (f32[2,8,2048]{2,1,0:T(8,128)S(1)}, bf16[128,256]{1,0:T(8,128)(2,1)S(1)}) custom-call(bf16[2,128,2048]{2,1,0:T(8,128)(2,1)S(1)} %get-tuple-element.53.turned_q.refs_2_, bf16[2,128,2048]{2,1,0:T(8,128)(2,1)S(1)} %get-tuple-element.54.turned_g.refs_3_, f32[2,8,2048]{2,1,0:T(8,128)S(1)} %attend_step3.1.earlier, ...), custom_call_target="tpu_custom_call", output_to_operand_aliasing={{0}: (2, {})} | custom-call | flops 1000 | bytes 1000 | tf_op jit(solution)/shard_map/attend_step4/pallas_call | solution.py:463
  39.3 2.8 %attend_grad_step4.1 = (bf16[528,256]{1,0:T(8,128)(2,1)S(1)}, f32[64,256]{1,0:T(8,128)S(1)}, bf16[48,256]{1,0:T(8,128)(2,1)S(1)}, f32[2,128,2048]{2,1,0:T(8,128)S(1)}) custom-call(bf16[2,2048,128]{2,1,0:T(8,128)(2,1)S(1)} %get-tuple-element.51.refs_0_, bf16[2,2048,128]{2,1,0:T(8,128)(2,1)S(1)} %get-tuple-element.52.refs_1_, ...), custom_call_target="tpu_custom_call" | custom-call | flops 1000 | bytes 1000 | tf_op jit(solution)/shard_map/attend_grad_step4/pallas_call | solution.py:505
  42.1 0.4 attend_grad_step3.1
  42.5 1.1 %collective-permute-start.7 = (bf16[560,256]{1,0:T(8,128)(2,1)S(1)}, bf16[560,256]{1,0:T(8,128)(2,1)S(1)}, u32[]{:S(2)}, u32[]{:S(2)}) collective-permute-start(bf16[560,256]{1,0:T(8,128)(2,1)S(1)} %get-tuple-element.72), channel_id=1, source_target_pairs={{0,1},{1,0},{2,3},{3,2},{4,5},{5,4},{6,7},{7,6},{8,9},{9,8},{10,11... | collective-permute-start | bytes 860168 | tf_op jit(solution)/shard_map/ppermute | solution.py:632
  43.6 2.0 %collective-permute-start.11 = (bf16[528,256]{1,0:T(8,128)(2,1)S(1)}, bf16[528,256]{1,0:T(8,128)(2,1)S(1)}, u32[]{:S(2)}, u32[]{:S(2)}) collective-permute-start(bf16[528,256]{1,0:T(8,128)(2,1)S(1)} %get-tuple-element.82), channel_id=1, source_target_pairs={{0,2},{1,3},{2,4},{3,5},{4,6},{5,7},{6,0},{7,1},{8,10},{9,11},{10,... | collective-permute-start | bytes 811016 | tf_op jit(solution)/shard_map/ppermute | solution.py:629
  45.6 0.3 attend_grad_step2.1
  45.9 4.7 %collective-permute-done.8.above = bf16[528,256]{1,0:T(8,128)(2,1)S(1)} collective-permute-done((bf16[528,256]{1,0:T(8,128)(2,1)S(1)}, bf16[528,256]{1,0:T(8,128)(2,1)S(1)}, u32[]{:S(2)}, u32[]{:S(2)}) %collective-permute-start.8) | collective-permute-done | bytes 270368 | tf_op jit(solution)/shard_map/ppermute | solution.py:629
  50.7 0.1 add_terms2.1
  50.8 1.4 %collective-permute-start.10 = (bf16[528,256]{1,0:T(8,128)(2,1)S(1)}, bf16[528,256]{1,0:T(8,128)(2,1)S(1)}, u32[]{:S(2)}, u32[]{:S(2)}) collective-permute-start(bf16[528,256]{1,0:T(8,128)(2,1)S(1)} %get-tuple-element.79), channel_id=1, source_target_pairs={{0,6},{1,7},{2,0},{3,1},{4,2},{5,3},{6,4},{7,5},{8,14},{9,15},{10,... | collective-permute-start | bytes 811016 | tf_op jit(solution)/shard_map/ppermute | solution.py:629
  52.1 1.0 %collective-permute-start.9 = (bf16[512,256]{1,0:T(8,128)(2,1)S(1)}, bf16[512,256]{1,0:T(8,128)(2,1)S(1)}, u32[]{:S(2)}, u32[]{:S(2)}) collective-permute-start(bf16[512,256]{1,0:T(8,128)(2,1)S(1)} %get-tuple-element.78), channel_id=1, source_target_pairs={{0,1},{1,0},{2,3},{3,2},{4,5},{5,4},{6,7},{7,6},{8,9},{9,8},{10,11... | collective-permute-start | bytes 786440 | tf_op jit(solution)/shard_map/ppermute | solution.py:632
  53.2 0.3 attend_grad_step1.1
  53.5 5.0 %collective-permute-done.9.side = bf16[512,256]{1,0:T(8,128)(2,1)S(1)} collective-permute-done((bf16[512,256]{1,0:T(8,128)(2,1)S(1)}, bf16[512,256]{1,0:T(8,128)(2,1)S(1)}, u32[]{:S(2)}, u32[]{:S(2)}) %collective-permute-start.9) | collective-permute-done | bytes 262176 | tf_op jit(solution)/shard_map/ppermute | solution.py:632
  58.5 0.0 collective-permute-done.11.refs_2_
  58.5 4.3 %collective-permute-done.10.above = bf16[528,256]{1,0:T(8,128)(2,1)S(1)} collective-permute-done((bf16[528,256]{1,0:T(8,128)(2,1)S(1)}, bf16[528,256]{1,0:T(8,128)(2,1)S(1)}, u32[]{:S(2)}, u32[]{:S(2)}) %collective-permute-start.10) | collective-permute-done | bytes 270368 | tf_op jit(solution)/shard_map/ppermute | solution.py:629
  62.9 0.2 add_terms1.1
  63.0 0.6 collective-permute-start.12
  63.6 2.0 %collective-permute-start.13 = (bf16[528,256]{1,0:T(8,128)(2,1)S(1)}, bf16[528,256]{1,0:T(8,128)(2,1)S(1)}, u32[]{:S(2)}, u32[]{:S(2)}) collective-permute-start(bf16[528,256]{1,0:T(8,128)(2,1)S(1)} %get-tuple-element.88), channel_id=1, source_target_pairs={{0,1},{1,0},{2,3},{3,2},{4,5},{5,4},{6,7},{7,6},{8,9},{9,8},{10,11... | collective-permute-start | bytes 811016 | tf_op jit(solution)/shard_map/ppermute | solution.py:632
  65.6 5.0 %attend_grad_step0.1 = (bf16[512,256]{1,0:T(8,128)(2,1)S(1)}, bf16[2,2048,128]{2,1,0:T(8,128)(2,1)}) custom-call(bf16[2,2048,128]{2,1,0:T(8,128)(2,1)S(1)} %get-tuple-element.51.refs_0_, bf16[2,2048,128]{2,1,0:T(8,128)(2,1)S(1)} %get-tuple-element.52.refs_1_, bf16[2,128,2048]{2,1,0:T(8,128)(2,1)S(1)} %get-tuple-element.53.turned_q.refs_2_, ...), custom_call_target="tpu_custom_call" | custom-call | flops 1000 | bytes 1000 | tf_op jit(solution)/shard_map/attend_grad_step0/pallas_call | solution.py:505
  70.6 1.5 %collective-permute-done.12.above = bf16[528,256]{1,0:T(8,128)(2,1)S(1)} collective-permute-done((bf16[528,256]{1,0:T(8,128)(2,1)S(1)}, bf16[528,256]{1,0:T(8,128)(2,1)S(1)}, u32[]{:S(2)}, u32[]{:S(2)}) %collective-permute-start.12) | collective-permute-done | bytes 270368 | tf_op jit(solution)/shard_map/ppermute | solution.py:629
  72.0 0.1 collective-permute-start.16
  72.1 2.3 %collective-permute-start.15 = (f32[16,256]{1,0:T(8,128)S(1)}, f32[16,256]{1,0:T(8,128)S(1)}, u32[]{:S(2)}, u32[]{:S(2)}) collective-permute-start(f32[16,256]{1,0:T(8,128)S(1)} %convert_add_fusion), channel_id=1, source_target_pairs={{0,16},{8,24},{16,0},{24,8},{1,17},{9,25},{17,1},{25,9},{2,18},{10... | collective-permute-start | bytes 49160 | tf_op jit(solution)/shard_map/ppermute | solution.py:704
  74.4 0.8 %add_terms0.1 = (bf16[512,128]{1,0:T(8,128)(2,1)}, bf16[512,128]{1,0:T(8,128)(2,1)}) custom-call(bf16[512,256]{1,0:T(8,128)(2,1)S(1)} %get-tuple-element.90.own, bf16[528,256]{1,0:T(8,128)(2,1)S(1)} %collective-permute-done.13.side, bf16[528,256]{1,0:T(8,128)(2,1)S(1)} %collective-permute-done.12.above), custom_call_target="tpu_custom_call" | custom-call | flops 1000 | bytes 1000 | tf_op jit(solution)/shard_map/add_terms0/pallas_call | solution.py:533
  75.2 0.1 collective-permute-done.16
  75.3 1.0 %collective-permute-done.15 = f32[16,256]{1,0:T(8,128)S(1)} collective-permute-done((f32[16,256]{1,0:T(8,128)S(1)}, f32[16,256]{1,0:T(8,128)S(1)}, u32[]{:S(2)}, u32[]{:S(2)}) %collective-permute-start.15) | collective-permute-done | bytes 16416 | tf_op jit(solution)/shard_map/ppermute | solution.py:704
  76.3 0.6 slice_add_fusion
  (11 shorter events, 0.0 us)
Async XLA Ops:
  2.4 13.3 %copy-start = (bf16[528,256]{1,0:T(8,128)(2,1)S(1)}, bf16[528,256]{1,0:T(8,128)(2,1)}, u32[]{:S(2)}) copy-start(bf16[528,256]{1,0:T(8,128)(2,1)} %get-tuple-element.55.refs_0_.refs_5_) | copy-start | bytes 811012
  2.4 11.8 %collective-permute-start = (bf16[528,256]{1,0:T(8,128)(2,1)}, bf16[528,256]{1,0:T(8,128)(2,1)S(1)}, u32[]{:S(2)}, u32[]{:S(2)}) collective-permute-start(bf16[528,256]{1,0:T(8,128)(2,1)} %get-tuple-element.55.refs_0_.refs_5_), channel_id=1, source_target_pairs={{0,2},{1,3},{2,4},{3,5},{4,6},{5,7},{6,0},{7,1},{8,10},{9,11},{10,... | collective-permute-start | bytes 811016 | tf_op jit(solution)/shard_map/ppermute | solution.py:629
  5.5 13.3 %collective-permute-start.2 = (bf16[528,256]{1,0:T(8,128)(2,1)}, bf16[528,256]{1,0:T(8,128)(2,1)S(1)}, u32[]{:S(2)}, u32[]{:S(2)}) collective-permute-start(bf16[528,256]{1,0:T(8,128)(2,1)} %get-tuple-element.55.refs_0_.refs_5_), channel_id=1, source_target_pairs={{0,1},{1,0},{2,3},{3,2},{4,5},{5,4},{6,7},{7,6},{8,9},{9,8},{10,11... | collective-permute-start | bytes 811016 | tf_op jit(solution)/shard_map/ppermute | solution.py:632
  7.0 1.2 %copy-start.1 = (bf16[2,256,8,128]{3,2,1,0:T(8,128)(2,1)S(1)}, bf16[2,256,8,128]{3,2,1,0:T(8,128)(2,1)}, u32[]{:S(2)}) copy-start(bf16[2,256,8,128]{3,2,1,0:T(8,128)(2,1)} %param.10) | copy-start | bytes 3145732
  8.2 1.2 %copy-start.2 = (bf16[2,256,8,128]{3,2,1,0:T(8,128)(2,1)S(1)}, bf16[2,256,8,128]{3,2,1,0:T(8,128)(2,1)}, u32[]{:S(2)}) copy-start(bf16[2,256,8,128]{3,2,1,0:T(8,128)(2,1)} %param.15) | copy-start | bytes 3145732
  9.4 0.7 copy-start.3
  14.2 9.5 %collective-permute-start.1 = (bf16[528,256]{1,0:T(8,128)(2,1)S(1)}, bf16[528,256]{1,0:T(8,128)(2,1)S(1)}, u32[]{:S(2)}, u32[]{:S(2)}) collective-permute-start(bf16[528,256]{1,0:T(8,128)(2,1)S(1)} %collective-permute-done.refs_1_.refs_6_), channel_id=1, source_target_pairs={{0,2},{1,3},{2,4},{3,5},{4,6},{5,7},{6,0},{7,1},{8,10},{9,11},{10,... | collective-permute-start | bytes 811016 | tf_op jit(solution)/shard_map/ppermute | solution.py:629
  14.2 14.5 %collective-permute-start.4 = (bf16[528,256]{1,0:T(8,128)(2,1)S(1)}, bf16[528,256]{1,0:T(8,128)(2,1)S(1)}, u32[]{:S(2)}, u32[]{:S(2)}) collective-permute-start(bf16[528,256]{1,0:T(8,128)(2,1)S(1)} %collective-permute-done.refs_1_.refs_6_), channel_id=1, source_target_pairs={{0,1},{1,0},{2,3},{3,2},{4,5},{5,4},{6,7},{7,6},{8,9},{9,8},{10,11... | collective-permute-start | bytes 811016 | tf_op jit(solution)/shard_map/ppermute | solution.py:632
  23.7 11.2 %collective-permute-start.3 = (bf16[528,256]{1,0:T(8,128)(2,1)S(1)}, bf16[528,256]{1,0:T(8,128)(2,1)S(1)}, u32[]{:S(2)}, u32[]{:S(2)}) collective-permute-start(bf16[528,256]{1,0:T(8,128)(2,1)S(1)} %collective-permute-done.1.refs_1_.refs_2_.refs_6_), channel_id=1, source_target_pairs={{0,2},{1,3},{2,4},{3,5},{4,6},{5,7},{6,0},{7,1},{8,10},{9,11},{10,... | collective-permute-start | bytes 811016 | tf_op jit(solution)/shard_map/ppermute | solution.py:629
  23.7 11.2 %collective-permute-start.5 = (bf16[528,256]{1,0:T(8,128)(2,1)S(1)}, bf16[528,256]{1,0:T(8,128)(2,1)S(1)}, u32[]{:S(2)}, u32[]{:S(2)}) collective-permute-start(bf16[528,256]{1,0:T(8,128)(2,1)S(1)} %collective-permute-done.1.refs_1_.refs_2_.refs_6_), channel_id=1, source_target_pairs={{0,1},{1,0},{2,3},{3,2},{4,5},{5,4},{6,7},{7,6},{8,9},{9,8},{10,11... | collective-permute-start | bytes 811016 | tf_op jit(solution)/shard_map/ppermute | solution.py:632
  25.0 12.0 %collective-permute-start.6 = (bf16[528,256]{1,0:T(8,128)(2,1)S(1)}, bf16[528,256]{1,0:T(8,128)(2,1)S(1)}, u32[]{:S(2)}, u32[]{:S(2)}) collective-permute-start(bf16[528,256]{1,0:T(8,128)(2,1)S(1)} %collective-permute-done.2.refs_0_.refs_4_.refs_5_), channel_id=1, source_target_pairs={{0,6},{1,7},{2,0},{3,1},{4,2},{5,3},{6,4},{7,5},{8,14},{9,15},{10,... | collective-permute-start | bytes 811016 | tf_op jit(solution)/shard_map/ppermute | solution.py:629
  42.5 8.2 %collective-permute-start.7 = (bf16[560,256]{1,0:T(8,128)(2,1)S(1)}, bf16[560,256]{1,0:T(8,128)(2,1)S(1)}, u32[]{:S(2)}, u32[]{:S(2)}) collective-permute-start(bf16[560,256]{1,0:T(8,128)(2,1)S(1)} %get-tuple-element.72), channel_id=1, source_target_pairs={{0,1},{1,0},{2,3},{3,2},{4,5},{5,4},{6,7},{7,6},{8,9},{9,8},{10,11... | collective-permute-start | bytes 860168 | tf_op jit(solution)/shard_map/ppermute | solution.py:632
  43.6 7.1 %collective-permute-start.8 = (bf16[528,256]{1,0:T(8,128)(2,1)S(1)}, bf16[528,256]{1,0:T(8,128)(2,1)S(1)}, u32[]{:S(2)}, u32[]{:S(2)}) collective-permute-start(bf16[528,256]{1,0:T(8,128)(2,1)S(1)} %get-tuple-element.73), channel_id=1, source_target_pairs={{0,6},{1,7},{2,0},{3,1},{4,2},{5,3},{6,4},{7,5},{8,14},{9,15},{10,... | collective-permute-start | bytes 811016 | tf_op jit(solution)/shard_map/ppermute | solution.py:629
  43.6 15.0 %collective-permute-start.11 = (bf16[528,256]{1,0:T(8,128)(2,1)S(1)}, bf16[528,256]{1,0:T(8,128)(2,1)S(1)}, u32[]{:S(2)}, u32[]{:S(2)}) collective-permute-start(bf16[528,256]{1,0:T(8,128)(2,1)S(1)} %get-tuple-element.82), channel_id=1, source_target_pairs={{0,2},{1,3},{2,4},{3,5},{4,6},{5,7},{6,0},{7,1},{8,10},{9,11},{10,... | collective-permute-start | bytes 811016 | tf_op jit(solution)/shard_map/ppermute | solution.py:629
  50.8 12.1 %collective-permute-start.10 = (bf16[528,256]{1,0:T(8,128)(2,1)S(1)}, bf16[528,256]{1,0:T(8,128)(2,1)S(1)}, u32[]{:S(2)}, u32[]{:S(2)}) collective-permute-start(bf16[528,256]{1,0:T(8,128)(2,1)S(1)} %get-tuple-element.79), channel_id=1, source_target_pairs={{0,6},{1,7},{2,0},{3,1},{4,2},{5,3},{6,4},{7,5},{8,14},{9,15},{10,... | collective-permute-start | bytes 811016 | tf_op jit(solution)/shard_map/ppermute | solution.py:629
  52.1 6.4 %collective-permute-start.9 = (bf16[512,256]{1,0:T(8,128)(2,1)S(1)}, bf16[512,256]{1,0:T(8,128)(2,1)S(1)}, u32[]{:S(2)}, u32[]{:S(2)}) collective-permute-start(bf16[512,256]{1,0:T(8,128)(2,1)S(1)} %get-tuple-element.78), channel_id=1, source_target_pairs={{0,1},{1,0},{2,3},{3,2},{4,5},{5,4},{6,7},{7,6},{8,9},{9,8},{10,11... | collective-permute-start | bytes 786440 | tf_op jit(solution)/shard_map/ppermute | solution.py:632
  63.0 9.0 %collective-permute-start.12 = (bf16[528,256]{1,0:T(8,128)(2,1)S(1)}, bf16[528,256]{1,0:T(8,128)(2,1)S(1)}, u32[]{:S(2)}, u32[]{:S(2)}) collective-permute-start(bf16[528,256]{1,0:T(8,128)(2,1)S(1)} %get-tuple-element.87), channel_id=1, source_target_pairs={{0,6},{1,7},{2,0},{3,1},{4,2},{5,3},{6,4},{7,5},{8,14},{9,15},{10,... | collective-permute-start | bytes 811016 | tf_op jit(solution)/shard_map/ppermute | solution.py:629
  63.6 8.5 %collective-permute-start.13 = (bf16[528,256]{1,0:T(8,128)(2,1)S(1)}, bf16[528,256]{1,0:T(8,128)(2,1)S(1)}, u32[]{:S(2)}, u32[]{:S(2)}) collective-permute-start(bf16[528,256]{1,0:T(8,128)(2,1)S(1)} %get-tuple-element.88), channel_id=1, source_target_pairs={{0,1},{1,0},{2,3},{3,2},{4,5},{5,4},{6,7},{7,6},{8,9},{9,8},{10,11... | collective-permute-start | bytes 811016 | tf_op jit(solution)/shard_map/ppermute | solution.py:632
  72.0 3.2 %collective-permute-start.16 = (f32[16,256]{1,0:T(8,128)S(1)}, f32[16,256]{1,0:T(8,128)S(1)}, u32[]{:S(2)}, u32[]{:S(2)}) collective-permute-start(f32[16,256]{1,0:T(8,128)S(1)} %convert_add_fusion), channel_id=1, source_target_pairs={{0,24},{8,16},{16,8},{24,0},{1,25},{9,17},{17,9},{25,1},{2,26},{10... | collective-permute-start | bytes 49160 | tf_op jit(solution)/shard_map/ppermute | solution.py:704
  72.1 4.2 %collective-permute-start.15 = (f32[16,256]{1,0:T(8,128)S(1)}, f32[16,256]{1,0:T(8,128)S(1)}, u32[]{:S(2)}, u32[]{:S(2)}) collective-permute-start(f32[16,256]{1,0:T(8,128)S(1)} %convert_add_fusion), channel_id=1, source_target_pairs={{0,16},{8,24},{16,0},{24,8},{1,17},{9,25},{17,1},{25,9},{2,18},{10... | collective-permute-start | bytes 49160 | tf_op jit(solution)/shard_map/ppermute | solution.py:704
  74.4 1.9 %collective-permute-start.14 = (f32[16,256]{1,0:T(8,128)S(1)}, f32[16,256]{1,0:T(8,128)S(1)}, u32[]{:S(2)}, u32[]{:S(2)}) collective-permute-start(f32[16,256]{1,0:T(8,128)S(1)} %convert_add_fusion), channel_id=1, source_target_pairs={{0,8},{8,0},{16,24},{24,16},{1,9},{9,1},{17,25},{25,17},{2,10},{10... | collective-permute-start | bytes 49160 | tf_op jit(solution)/shard_map/ppermute | solution.py:704
